TPU v7x, 256 devices: a whole 4x4x8 slice. The times are simulated.
256 devices in a mesh: blk: 32 (over y_lo, z, core), dp: 8 (over x, y_hi).
Axes of the slice: x: 4, y: 4 (y_hi: 2, y_lo: 2; y = y_hi * 2 + y_lo), z: 8, core: 2. Of those that a mesh axis runs over, the one named last changes fastest.
Arguments:
- residuals: bfloat16 [32768, 768], P(('blk', 'dp')), may hold values from -130 to 130
- codebook: bfloat16 [24576, 768], P('blk'), may hold values from -9 to 9
- section_codes: int32 [32768], P(('blk', 'dp')), may hold values from 0 to 1023, as said below
- code_owner: int32 [1024], replicated, may hold values from 0 to 31, as said below
Outputs:
- new_codebook: float32 [24576, 768], P('blk')
- code_shift: float32 [2048, 768], P('blk')
Inputs may be any that keep to these rules, and one draw needn't show every extreme that they name: `section_codes`: among the rows of one device, at most 12 have section-one codes owned by one codeword block, and in every device's rows some block is named exactly 12 times. `code_owner`: each codeword block owns at least one and at most 64 section-one codes; some block owns exactly 64.
All inputs are finite; a program needn't handle non-finite values.
Results may differ from a plain program's by a relative error of at most 0.002.
Values may be sent and summed in bfloat16 or wider, within the bound.
No kernel may reach another device: no remote copies, remote signals or barrier semaphores. Data moves between devices by JAX's collectives and lax.ppermute only.
A program may use at most 128 MiB of HBM per device.

v0:
```python
import math

import jax
import jax.numpy as jnp
from jax import lax
from jax.sharding import PartitionSpec as P

SLOTS = 64


prior_weight = 0.5


def merged(value, axis, join):
    pieces = jax.tree.map(lambda part: lax.all_gather(part, axis), value)
    head = jax.tree.map(lambda part: part[0], pieces)
    tail = jax.tree.map(lambda part: part[1:], pieces)
    running, _ = lax.scan(lambda running, section: (join(running, section), None), head, tail)
    return running


def score_block(rows, codebook, half_norm):
    raw = lax.dot_general(
        rows, codebook, (((1,), (1,)), ((), ())), preferred_element_type=jnp.float32
    )
    return (raw - half_norm[None, :]) * (2.0 / math.sqrt(rows.shape[1]))


def block_rows():
    return 512


def row_stats(rows, codebook, half_norm):
    count = rows.shape[0]
    size = block_rows()
    stacked = rows.reshape(count // size, size, rows.shape[1])

    def one_block(block):
        scores = score_block(block, codebook, half_norm)
        top = jnp.max(scores, axis=1)
        total = jnp.sum(jnp.exp(scores - top[:, None]), axis=1)
        return (top, total)

    top, total = lax.map(one_block, stacked)
    return (top.reshape(-1), total.reshape(-1))


def accumulate(carry, rows, top, total, codebook, half_norm):
    count = rows.shape[0]
    size = block_rows()
    stacked = rows.reshape(count // size, size, rows.shape[1])
    tops = top.reshape(count // size, size)
    totals = total.reshape(count // size, size)

    def add_weights(state, block, scores, block_top, block_total):
        weights = (jnp.exp(scores - block_top[:, None]) / block_total[:, None]).astype(jnp.bfloat16)
        weighted = state[0] + lax.dot_general(
            weights, block, (((0,), (0,)), ((), ())), preferred_element_type=jnp.float32
        )
        mass = state[1] + jnp.sum(weights.astype(jnp.float32), axis=0)
        return (weighted, mass)

    def fresh_block(state, item):
        block, block_top, block_total = item
        scores = score_block(block, codebook, half_norm)
        return (add_weights(state, block, scores, block_top, block_total), None)

    result, _ = lax.scan(fresh_block, carry, (stacked, tops, totals))
    return result


def combine_stats(first, second):
    top = jnp.maximum(first[0], second[0])
    total = first[1] * jnp.exp(first[0] - top) + second[1] * jnp.exp(second[0] - top)
    return (top, total)


def local(residuals, codebook, section_codes, code_owner):
    nblk = lax.axis_size("blk")
    row_count, width = residuals.shape
    half_norm = 0.5 * jnp.sum(jnp.square(codebook.astype(jnp.float32)), axis=1)
    top, total = row_stats(
        lax.all_gather(residuals, "blk", axis=0, tiled=True), codebook, half_norm
    )
    local_stats = (top, total)
    top_all, total_all = merged(local_stats, "blk", combine_stats)
    zero_sums = (
        jnp.zeros((codebook.shape[0], width), jnp.float32),
        jnp.zeros((codebook.shape[0],), jnp.float32),
    )
    top = top_all
    total = total_all
    weighted, mass = accumulate(
        zero_sums,
        lax.all_gather(residuals, "blk", axis=0, tiled=True),
        top,
        total,
        codebook,
        half_norm,
    )
    code_count = code_owner.shape[0]
    owner_hot = (code_owner[:, None] == jnp.arange(nblk, dtype=jnp.int32)[None, :]).astype(
        jnp.int32
    )
    before = jnp.cumsum(owner_hot, axis=0) - owner_hot
    rank = jnp.sum(before * owner_hot, axis=1)
    code_slot = code_owner * SLOTS + rank
    code_hit = section_codes[:, None] == jnp.arange(code_count, dtype=jnp.int32)[None, :]
    row_slot = jnp.sum(jnp.where(code_hit, code_slot[None, :], 0), axis=1)
    capacity = max(2, 3 * row_count // nblk)
    target = row_slot // SLOTS
    local_slot = row_slot - target * SLOTS
    target_hot = (target[:, None] == jnp.arange(nblk, dtype=jnp.int32)[None, :]).astype(jnp.int32)
    earlier = jnp.cumsum(target_hot, axis=0) - target_hot
    position = jnp.sum(earlier * target_hot, axis=1)
    flat_index = target * capacity + position
    row_buffer = jnp.zeros((nblk * capacity, width), jnp.bfloat16).at[flat_index].set(residuals)
    slot_hot = (local_slot[:, None] == jnp.arange(SLOTS, dtype=jnp.int32)[None, :]).astype(
        jnp.bfloat16
    )
    tag_buffer = jnp.zeros((nblk * capacity, SLOTS), jnp.bfloat16).at[flat_index].set(slot_hot)
    got_rows, got_tags = (
        lax.all_to_all(
            row_buffer.reshape(nblk, capacity, width),
            "blk",
            split_axis=0,
            concat_axis=0,
            tiled=True,
        ),
        lax.all_to_all(
            tag_buffer.reshape(nblk, capacity, SLOTS),
            "blk",
            split_axis=0,
            concat_axis=0,
            tiled=True,
        ),
    )
    tags_flat = got_tags.reshape(nblk * capacity, SLOTS)
    shift_sum = lax.dot_general(
        tags_flat,
        got_rows.reshape(nblk * capacity, width),
        (((0,), (0,)), ((), ())),
        preferred_element_type=jnp.float32,
    )
    shift_count = jnp.sum(tags_flat.astype(jnp.float32), axis=0)
    weighted, mass, shift_sum, shift_count = lax.psum(
        (weighted, mass, shift_sum, shift_count), "dp"
    )
    new_codebook = (weighted + prior_weight * codebook.astype(jnp.float32)) / (mass + prior_weight)[
        :, None
    ]
    code_shift = shift_sum / (shift_count + 1.0)[:, None]
    return (new_codebook, code_shift)


def solution(mesh):
    in_specs = (P(("blk", "dp"), None), P("blk", None), P(("blk", "dp")), P())
    out_specs = (P("blk", None), P("blk", None))
    return jax.shard_map(local, mesh=mesh, in_specs=in_specs, out_specs=out_specs, check_vma=False)
```

profile of v0, /device:TPU:1, one launch (start us, length us, event | category | flops | bytes accessed | tf_op | source)
XLA Modules:
  0.0 415.2 jit_solution(8335260162383934717)
XLA Ops:
  8.6 9.0 %reduce-window.6 = s32[32,8,128]{2,1,0:T(8,128)S(1)} reduce-window(s32[32,8,128]{2,1,0:T(8,128)S(1)} %fusion.18, s32[]{:T(128)} %constant.71.clone.1), window={size=1x1x128 pad=0_0x0_0x127_0}, to_apply=%region_12.13 | reduce-window | flops 4161536 | bytes 262148 | tf_op jit(solution)/shard_map/reduce-window
  22.6 11.1 %all-to-all-start = ((bf16[32,2,384]{2,1,0:T(2,128)(2,1)}), bf16[32,2,384]{2,1,0:T(2,128)(2,1)S(1)}, u32[]{:S(2)}, u32[]{:S(2)}) async-start(bf16[32,2,384]{2,1,0:T(2,128)(2,1)} %reshape.162), calls=%async_computation | async-start | bytes 98304 | tf_op jit(solution)/shard_map/all_to_all | solution.py:130
  33.8 1.7 scatter_custom_fusion.1
  36.5 5.5 %all-to-all-done = bf16[32,2,384]{2,1,0:T(2,128)(2,1)S(1)} async-done(((bf16[32,2,384]{2,1,0:T(2,128)(2,1)}), bf16[32,2,384]{2,1,0:T(2,128)(2,1)S(1)}, u32[]{:S(2)}, u32[]{:S(2)}) %all-to-all-start) | async-done | bytes 49184 | tf_op jit(solution)/shard_map/all_to_all | solution.py:130
  42.0 4.7 %all-to-all-start.1 = ((bf16[32,12,768]{2,1,0:T(8,128)(2,1)}), bf16[32,12,768]{2,1,0:T(8,128)(2,1)S(1)}, u32[]{:S(2)}, u32[]{:S(2)}) async-start(bf16[32,12,768]{2,1,0:T(8,128)(2,1)} %reshape.128), calls=%async_computation.1 | async-start | bytes 1572864 | tf_op jit(solution)/shard_map/all_to_all | solution.py:123
  46.8 1.6 fusion.9
  48.5 27.0 %all-to-all-done.1 = bf16[32,12,768]{2,1,0:T(8,128)(2,1)S(1)} async-done(((bf16[32,12,768]{2,1,0:T(8,128)(2,1)}), bf16[32,12,768]{2,1,0:T(8,128)(2,1)S(1)}, u32[]{:S(2)}, u32[]{:S(2)}) %all-to-all-start.1) | async-done | bytes 589856 | tf_op jit(solution)/shard_map/all_to_all | solution.py:123
  76.5 20.7 %all-gather.4.cloned.1.call-done = bf16[4096,768]{1,0:T(8,128)(2,1)} async-done(((bf16[128,768]{1,0:T(8,128)(2,1)}), bf16[4096,768]{1,0:T(8,128)(2,1)}) %all-gather.4.cloned.1.call-update) | async-done | bytes 6291472 | tf_op jit(solution)/shard_map/all_gather | solution.py:95
  97.2 33.8 %while.37 = (s32[]{:T(128)}, f32[8,512]{1,0:T(8,128)S(1)}, f32[8,512]{1,0:T(8,128)}, bf16[8,512,768]{2,1,0:T(8,128)(2,1)}, bf16[768,768]{1,0:T(8,128)(2,1)}, /*index=5*/f32[768]{0:T(1024)S(1)}, s32[]{:T(128)}, s32[]{:T(128)}) while((s32[]{:T(128)}, f32[8,512]{1,0:T(8,128)S(1)}, f32[8,512]{1,0:T(8,128)}, bf16[8,512,768]{2,1,0:T(8,128)(2,1)}, ...), condition=%wide.region_4.5_spmd, body=%wide.region_1.4_spmd.sunk | while | flops 605944832 | bytes 5129821 | solution.py:44
  97.2 2.4 fusion.37
  100.1 1.3 dynamic_update_slice.10
  101.4 2.4 fusion.37
  104.3 1.3 dynamic_update_slice.10
  105.7 2.4 fusion.37
  108.5 1.3 dynamic_update_slice.10
  109.9 2.4 fusion.37
  112.7 1.3 dynamic_update_slice.10
  114.1 2.4 fusion.37
  117.0 1.3 dynamic_update_slice.10
  118.3 2.4 fusion.37
  122.6 2.4 fusion.37
  125.4 1.3 dynamic_update_slice.10
  126.8 2.4 fusion.37
  131.6 34.3 %all-gather = f32[32,1,4096]{2,1,0:T(1,128)S(1)} all-gather(f32[1,1,4096]{2,1,0:T(1,128)S(1)} %reshape.145), channel_id=1, replica_groups=mesh['blk'=32,'dp'=8] {'blk'}, dimensions={0}, use_global_device_ids=true | all-gather | bytes 540672 | tf_op jit(solution)/shard_map/all_gather | solution.py:15
  166.0 32.1 %all-gather.1 = f32[32,1,4096]{2,1,0:T(1,128)S(1)} all-gather(f32[1,1,4096]{2,1,0:T(1,128)S(1)} %reshape.147), channel_id=1, replica_groups=mesh['blk'=32,'dp'=8] {'blk'}, dimensions={0}, use_global_device_ids=true | all-gather | bytes 540672 | tf_op jit(solution)/shard_map/all_gather | solution.py:15
  199.5 30.3 %while.38 = (s32[]{:T(128)}, f32[4096]{0:T(1024)S(1)}, f32[4096]{0:T(1024)S(1)}, f32[31,4096]{1,0:T(8,128)}, f32[31,4096]{1,0:T(8,128)S(1)}, /*index=5*/s32[]{:T(128)}) while((s32[]{:T(128)}, f32[4096]{0:T(1024)S(1)}, f32[4096]{0:T(1024)S(1)}, f32[31,4096]{1,0:T(8,128)}, f32[31,4096]{1,0:T(8,128)S(1)}, /*index=5*/s32[]{:T(128)}) %tuple.87), condition=%wide.region_6.7_spmd, body=%wide.region_5.6_spmd.sunk | while | flops 24578 | bytes 163913 | solution.py:18
  229.9 44.6 %while.39 = (s32[]{:T(128)}, f32[768,768]{1,0:T(8,128)S(1)}, f32[768]{0:T(1024)}, bf16[8,512,768]{2,1,0:T(8,128)(2,1)}, bf16[768,768]{1,0:T(8,128)(2,1)}, /*inde...) while((s32[]{:T(128)}, f32[768,768]{1,0:T(8,128)S(1)}, ...), condition=%wide.region_9.10_spmd.clone, body=%wide.region_7.9_spmd.clone.sunk | while | flops 1211892480 | bytes 9098412 | solution.py:68
  229.9 2.4 convert_reduce_fusion.3
  232.3 2.5 select_add_fusion.4
  235.5 2.4 convert_reduce_fusion.3
  237.9 2.5 select_add_fusion.4
  241.0 2.4 convert_reduce_fusion.3
  243.5 2.5 select_add_fusion.4
  246.6 2.4 convert_reduce_fusion.3
  249.1 2.5 select_add_fusion.4
  252.2 2.4 convert_reduce_fusion.3
  254.6 2.5 select_add_fusion.4
  257.8 2.4 convert_reduce_fusion.3
  260.2 2.5 select_add_fusion.4
  263.3 2.4 convert_reduce_fusion.3
  265.8 2.5 select_add_fusion.4
  268.9 2.4 convert_reduce_fusion.3
  271.4 2.5 select_add_fusion.4
  274.5 1.4 copy-done
  276.0 21.1 %all-reduce = (f32[768]{0:T(1024)S(1)}, f32[64]{0:T(128)S(1)}) all-reduce(f32[768]{0:T(1024)S(1)} %copy-done.3, f32[64]{0:T(128)S(1)} %convert_reduce_fusion.1), channel_id=1, replica_groups=mesh['blk'=32,'dp'=8] {'dp'}, use_global_device_ids=true, to_apply=%region_11.12 | all-reduce | flops 832 | bytes 6656 | tf_op jit(solution)/shard_map/psum | solution.py:146
  297.2 105.8 %all-reduce.4.cloned.1.call-done = (f32[768,768]{1,0:T(8,128)}, f32[64,768]{1,0:T(8,128)}) async-done(((f32[768,768]{1,0:T(8,128)}, f32[64,768]{1,0:T(8,128)}), (f32[768,768]{1,0:T(8,128)}, f32[64,768]{1,0:T(8,128)})) %all-reduce.4.cloned.1.call-update) | async-done | bytes 2555920 | tf_op jit(solution)/shard_map/psum | solution.py:146
  402.9 1.7 broadcast_divide_fusion
  404.6 3.7 fusion.11
  (178 shorter events, 51.4 us)
Async XLA Ops:
  7.2 90.1 %all-gather.4.cloned.1.call-start = ((), (), s32[]{:S(2)}) async-start(), calls=%async_computation.2 | async-start | bytes 6488064 | tf_op jit(solution)/shard_map/all_gather | solution.py:95
  22.6 19.4 %all-to-all-start = ((bf16[32,2,384]{2,1,0:T(2,128)(2,1)}), bf16[32,2,384]{2,1,0:T(2,128)(2,1)S(1)}, u32[]{:S(2)}, u32[]{:S(2)}) async-start(bf16[32,2,384]{2,1,0:T(2,128)(2,1)} %reshape.162), calls=%async_computation | async-start | bytes 98304 | tf_op jit(solution)/shard_map/all_to_all | solution.py:130
  42.0 33.5 %all-to-all-start.1 = ((bf16[32,12,768]{2,1,0:T(8,128)(2,1)}), bf16[32,12,768]{2,1,0:T(8,128)(2,1)S(1)}, u32[]{:S(2)}, u32[]{:S(2)}) async-start(bf16[32,12,768]{2,1,0:T(8,128)(2,1)} %reshape.128), calls=%async_computation.1 | async-start | bytes 1572864 | tf_op jit(solution)/shard_map/all_to_all | solution.py:123
  46.7 356.3 %all-reduce.4.cloned.1.call-start = ((), (), s32[]{:S(2)}) async-start(), calls=%async_computation.3 | async-start | bytes 5111808 | tf_op jit(solution)/shard_map/psum | solution.py:146
  131.0 0.6 copy-start.5
  131.0 34.9 %copy-start.4 = (f32[8,512]{1,0:T(8,128)S(1)}, f32[8,512]{1,0:T(8,128)}, u32[]{:S(2)}) copy-start(f32[8,512]{1,0:T(8,128)} %get-tuple-element.107) | copy-start | bytes 49156
  232.3 2.5 copy-start.1
  234.9 0.6 copy-start.2
  237.9 2.5 copy-start.1
  240.4 0.6 copy-start.2
  243.5 2.5 copy-start.1
  246.0 0.6 copy-start.2
  249.1 2.5 copy-start.1
  251.6 0.6 copy-start.2
  254.6 2.5 copy-start.1
  257.2 0.6 copy-start.2
  260.2 2.5 copy-start.1
  262.7 0.6 copy-start.2
  265.8 2.5 copy-start.1
  268.3 0.6 copy-start.2
  271.4 2.5 copy-start.1
  273.9 0.6 copy-start.2
  274.5 1.4 copy-start
  274.5 1.5 copy-start.3
Sparse Core Ops, SparseCore 0:
  9.9 87.3 all-gather.3
  276.0 126.8 all-reduce.3
where the time goes:
time: 419 us; the launch traced here: 415 us
  waiting for transfers between devices  160 us (38%)
  blocking collectives  87.5 us (21%)
  matrix products  59.7 us (14%)
  local copies, waits for them, and re-layouts  52 us (12%)
  other arithmetic  24.8 us (6%)
  starting transfers between devices  15.9 us (4%)
  between operations  14.3 us (3%)
    psum x1, waiting for transfers between devices, local(): lax.psum((weighted, mass, shift_sum, shift_count), 'dp')  106 us
    all_gather x2, blocking collectives, merged(): pieces = jax.tree.map(lambda part: lax.all_gather(part, axis), value)  66.4 us
    dot_general x16, matrix products, score_block(): lax.dot_general(rows, codebook, (((1,), (1,)), ((), ())), preferred_eleme...  38.8 us
    dynamic_slice x31, local copies, waits for them, and re-layouts, merged(): lax.scan(lambda running, section: (join(running, section), None), head, t...  28.9 us
    all_to_all x1, waiting for transfers between devices, local(): lax.all_to_all(row_buffer.reshape(nblk, capacity, width), 'blk', split_ax...  27 us
    psum x1, blocking collectives, local(): lax.psum((weighted, mass, shift_sum, shift_count), 'dp')  21.1 us
    all_gather x1, waiting for transfers between devices, local(): lax.all_gather(residuals, 'blk', axis=0, tiled=True)  20.7 us
    dot_general x8, matrix products, add_weights(): lax.dot_general(weights, block, (((0,), (0,)), ((), ())), preferred_eleme...  19.9 us
  transfers between devices with their start and end apart: 4, of which 4 were waited for; matrix products, arithmetic and copies ran while one was open for 5% of the time, Pallas kernels for 0%

commit v1 on v0

v1 whole, which is shorter than its diff:
```python
import functools
import math

import jax
import jax.numpy as jnp
from jax import lax
from jax.experimental import pallas as pl
from jax.experimental.pallas import tpu as pltpu
from jax.sharding import PartitionSpec as P

SLOTS = 64
X, Y, Z, C = 4, 4, 8, 2
PEERS = X * Y // 2
AXES = ("blk", "dp")
PRIOR = 0.5
MIB = 1 << 20


def place(x, y, z, c):
    return ((y % 2 * Z + z) * C + c) * PEERS + x * 2 + y // 2


def chips():
    for x in range(X):
        for y in range(Y):
            for z in range(Z):
                for c in range(C):
                    yield x, y, z, c


def shifted(value, dy=0, dz=0, dc=0):
    pairs = [
        (place(x, y, z, c), place(x, (y + dy) % Y, (z + dz) % Z, (c + dc) % C)) for x, y, z, c in chips()
    ]
    return lax.ppermute(value, AXES, pairs)


def z_partner(value, bit):
    pairs = [(place(x, y, z, c), place(x, y, z ^ bit, c)) for x, y, z, c in chips()]
    return lax.ppermute(value, AXES, pairs)


def score_kernel(count, *refs):
    codebook, half_norm = refs[:2]
    rows = refs[2 : 2 + count]
    expo, stats = refs[2 + count :]
    factor = 2.0 / math.sqrt(codebook.shape[1])
    at = 0
    for block in rows:
        n = block.shape[0]
        raw = lax.dot_general(
            codebook[...], block[...], (((1,), (1,)), ((), ())), preferred_element_type=jnp.float32
        )
        scores = (raw - half_norm[...]) * factor
        top = jnp.max(scores, axis=0, keepdims=True)
        value = jnp.exp(scores - top)
        expo[:, at : at + n] = value
        stats[0:1, at : at + n] = top
        stats[1:2, at : at + n] = jnp.sum(value, axis=0, keepdims=True)
        at += n


def score_rows(codebook, half_norm, rows):
    k, width = codebook.shape
    total = sum(r.shape[0] for r in rows)
    return pl.pallas_call(
        functools.partial(score_kernel, len(rows)),
        out_shape=(
            jax.ShapeDtypeStruct((k, total), jnp.float32),
            jax.ShapeDtypeStruct((2, total), jnp.float32),
        ),
        compiler_params=pltpu.CompilerParams(vmem_limit_bytes=24 * MIB),
        cost_estimate=pl.CostEstimate(
            flops=2 * k * width * total, bytes_accessed=2 * k * width + 4 * k * total, transcendentals=k * total
        ),
    )(codebook, half_norm, *rows)


def sum_kernel(layout, *refs):
    groups = len(layout)
    count = sum(len(g) for g in layout)
    expos = refs[:groups]
    rows = refs[groups : groups + count]
    scale, slots, weighted, mass, shift, hits = refs[groups + count :]
    k = weighted.shape[0]
    tile = 256

    def pieces():
        at, i = 0, 0
        for g, sizes in enumerate(layout):
            inner = 0
            for n in sizes:
                yield g, inner, at, n, rows[i]
                inner, at, i = inner + n, at + n, i + 1

    def folded(w):
        w = w.astype(jnp.float32)
        return sum(w[:, j : j + 128] for j in range(0, w.shape[1], 128))

    for t in range(0, k, tile):
        total = jnp.zeros((tile, weighted.shape[1]), jnp.float32)
        heavy = jnp.zeros((tile, 128), jnp.float32)
        for g, inner, at, n, block in pieces():
            w = (expos[g][t : t + tile, inner : inner + n] * scale[0:1, at : at + n]).astype(jnp.bfloat16)
            total += jnp.dot(w, block[...], preferred_element_type=jnp.float32)
            heavy += folded(w)
        weighted[t : t + tile, :] = total
        mass[t : t + tile, :] = jnp.sum(heavy, axis=1, keepdims=True)
    total = jnp.zeros(shift.shape, jnp.float32)
    heavy = jnp.zeros((SLOTS, 128), jnp.float32)
    for g, inner, at, n, block in pieces():
        want = lax.broadcasted_iota(jnp.int32, (SLOTS, n), 0)
        hot = jnp.where(want == slots[0:1, at : at + n], 1.0, 0.0).astype(jnp.bfloat16)
        total += jnp.dot(hot, block[...], preferred_element_type=jnp.float32)
        heavy += folded(hot)
    shift[...] = total
    hits[...] = jnp.sum(heavy, axis=1, keepdims=True)


def sum_rows(expos, rows, scale, slots):
    k = expos[0].shape[0]
    flat = [r for group in rows for r in group]
    width = flat[0].shape[1]
    total = sum(r.shape[0] for r in flat)
    return pl.pallas_call(
        functools.partial(sum_kernel, [[r.shape[0] for r in group] for group in rows]),
        out_shape=(
            jax.ShapeDtypeStruct((k, width), jnp.float32),
            jax.ShapeDtypeStruct((k, 1), jnp.float32),
            jax.ShapeDtypeStruct((SLOTS, width), jnp.float32),
            jax.ShapeDtypeStruct((SLOTS, 1), jnp.float32),
        ),
        compiler_params=pltpu.CompilerParams(vmem_limit_bytes=24 * MIB),
        cost_estimate=pl.CostEstimate(
            flops=2 * (k + SLOTS) * width * total, bytes_accessed=4 * k * total + 2 * width * total, transcendentals=0
        ),
    )(*expos, *flat, scale, slots)


def combine(first, second):
    top = jnp.maximum(first[0], second[0])
    total = first[1] * jnp.exp(first[0] - top) + second[1] * jnp.exp(second[0] - top)
    return jnp.stack([top, total, first[2] + second[2]])


def row_slots(section_codes, code_owner):
    codes = code_owner.shape[0]
    index = jnp.arange(codes, dtype=jnp.int32)
    same = (code_owner[:, None] == code_owner[None, :]) & (index[None, :] < index[:, None])
    code_slot = code_owner * SLOTS + jnp.sum(same.astype(jnp.int32), axis=1)
    hit = section_codes[:, None] == index[None, :]
    return jnp.sum(jnp.where(hit, code_slot[None, :], 0), axis=1)


def halved(rows):
    size = jnp.max(jnp.abs(rows), axis=-1, keepdims=True)
    exponent = jnp.clip(jnp.ceil(jnp.log2(jnp.maximum(size, 1e-30))), -100.0, 100.0)
    return (rows * jnp.exp2(-exponent)).astype(jnp.float16), exponent


def as_row(values, width):
    pad = [(0, 0)] * (values.ndim - 1) + [(0, width - values.shape[-1])]
    return jnp.pad(values, pad)[..., None, :].astype(jnp.float16)


def local(residuals, codebook, section_codes, code_owner):
    blk = lax.axis_index("blk")
    peer = lax.axis_index("dp")
    z, core = blk // C % Z, blk % C
    count, width = residuals.shape
    k = codebook.shape[0]
    half = count // 2

    start = jnp.concatenate(
        [residuals, shifted(residuals[:half], dy=1), shifted(residuals[half:], dy=-1)]
    )
    side = start.shape[0]
    up, down = [start], [start]
    for _ in range(Z // 2 - 1):
        up.append(shifted(up[-1], dz=1))
        down.append(shifted(down[-1], dz=-1))
    up.append(shifted(up[-1][: side // 2], dz=1))
    down.append(shifted(down[-1][side // 2 :], dz=-1))
    rounds = [[start]] + [[up[i], down[i]] for i in range(1, Z // 2 + 1)]
    rows = [[r for own in group for r in (own, shifted(own, dc=1))] for group in rounds]

    half_norm = 0.5 * jnp.sum(jnp.square(codebook.astype(jnp.float32)), axis=1, keepdims=True)
    scored = [score_rows(codebook, half_norm, group) for group in rows]
    expos = [s[0] for s in scored]

    by_z = [None] * Z
    by_z[0] = scored[0][1].reshape(2, 1, C, side)
    for i in range(1, Z // 2):
        pair = scored[i][1].reshape(2, 2, C, side)
        by_z[Z - i], by_z[i] = pair[:, :1], pair[:, 1:]
    last = scored[Z // 2][1].reshape(2, 2, C, side // 2)
    by_z[Z // 2] = jnp.concatenate([last[:, 0], last[:, 1]], axis=2)[:, None]
    near = jnp.concatenate(by_z, axis=1)

    def to_absolute(a):
        a = lax.dynamic_slice_in_dim(jnp.concatenate([a, a], axis=1), (Z - z) % Z, Z, axis=1)
        return jnp.where(core == 0, a, a[:, :, ::-1])

    def to_near(a):
        a = lax.dynamic_slice_in_dim(jnp.concatenate([a, a], axis=1), z, Z, axis=1)
        return jnp.where(core == 0, a, a[:, :, ::-1])

    slots = row_slots(section_codes, code_owner).astype(jnp.float32)
    own = (jnp.arange(Z)[:, None, None] == z) & (jnp.arange(C)[None, :, None] == core)
    mine = jnp.where(own, jnp.pad(slots, (0, side - count))[None, None, :], 0.0)
    stats = jnp.concatenate([to_absolute(near), mine[None]])

    a, b, c, d = (stats[..., i * half : (i + 1) * half] for i in range(4))
    from_up = shifted(jnp.concatenate([b, c], axis=-1), dy=-1)
    from_down = shifted(jnp.concatenate([a, d], axis=-1), dy=1)
    stats = combine(
        stats,
        jnp.concatenate(
            [from_up[..., half:], from_down[..., half:], from_down[..., :half], from_up[..., :half]], axis=-1
        ),
    )
    stats = combine(stats, shifted(stats, dc=1))
    for bit in (1, 2, 4):
        stats = combine(stats, z_partner(stats, bit))

    stats = to_near(stats)
    scale = jnp.exp(near[0] - stats[0]) / stats[1]
    slot_of = stats[2].astype(jnp.int32) - blk * SLOTS

    def in_order(a):
        out = [a[0].reshape(-1)]
        for i in range(1, Z // 2):
            out += [a[Z - i].reshape(-1), a[i].reshape(-1)]
        far = a[Z // 2]
        return jnp.concatenate(out + [far[:, : side // 2].reshape(-1), far[:, side // 2 :].reshape(-1)])[None]

    weighted, mass, shift, hits = sum_rows(expos, rows, in_order(scale), in_order(slot_of))

    part, slot_part = k // PEERS, SLOTS // PEERS
    sums = jnp.concatenate(
        [weighted.reshape(PEERS, part, width), shift.reshape(PEERS, slot_part, width)], axis=1
    )
    counts = jnp.concatenate([mass.reshape(PEERS, part), hits.reshape(PEERS, slot_part)], axis=1)
    packed, exponent = halved(sums)
    high = lax.reduce_precision(counts, 5, 10)
    lines = [as_row(v, width) for v in (exponent[..., 0], high, counts - high)]
    got = lax.all_to_all(
        jnp.concatenate([packed, *lines], axis=1), "dp", split_axis=0, concat_axis=0, tiled=True
    ).astype(jnp.float32)
    both = part + slot_part
    sums = jnp.sum(got[:, :both] * jnp.exp2(got[:, both, :both])[..., None], axis=0)
    counts = jnp.sum(got[:, both + 1, :both] + got[:, both + 2, :both], axis=0)[:, None]
    prior = PRIOR * lax.dynamic_slice_in_dim(codebook, peer * part, part).astype(jnp.float32)
    result = jnp.concatenate(
        [
            (sums[:part] + prior) / (counts[:part] + PRIOR),
            sums[part:] / (counts[part:] + 1.0),
        ]
    )
    packed, exponent = halved(result)
    sent = jnp.concatenate([packed, as_row(exponent[:, 0], width)])
    got = lax.all_to_all(
        jnp.broadcast_to(sent[None], (PEERS, *sent.shape)), "dp", split_axis=0, concat_axis=0, tiled=True
    ).astype(jnp.float32)
    result = got[:, :both] * jnp.exp2(got[:, both, :both])[..., None]
    return result[:, :part].reshape(k, width), result[:, part:].reshape(SLOTS, width)


def solution(mesh):
    in_specs = (P(("blk", "dp"), None), P("blk", None), P(("blk", "dp")), P())
    out_specs = (P("blk", None), P("blk", None))
    return jax.shard_map(local, mesh=mesh, in_specs=in_specs, out_specs=out_specs, check_vma=False)
```

time: 419 us -> 184 us (0.44)
  waiting for transfers between devices: 160 us -> 37.7 us
  blocking collectives: 87.5 us -> 24.9 us
  matrix products: 59.7 us -> 0 us
  starting transfers between devices: 15.9 us -> 41.7 us
  Pallas kernels: 0 us -> 20.1 us
  between operations: 14.3 us -> 1.47 us
  local copies, waits for them, and re-layouts: 52 us -> 40.3 us
  other arithmetic: 24.8 us -> 14.6 us
    psum x1 -> x0, waiting for transfers between devices: 106 us -> none  [local(): lax.psum((weighted, mass, shift_sum, shift_count), 'dp')]
    all_gather x2 -> x0, blocking collectives: 66.4 us -> none  [merged(): pieces = jax.tree.map(lambda part: lax.all_gather(part, axis), value)]
    dot_general x25 -> x0, matrix products: 59.7 us -> none  [the longest x16 38.8 us: score_block(): lax.dot_general(rows, codebook, (((1,), (1,)), ((), ())), preferred_eleme...]
    ppermute x0 -> x25, starting transfers between devices: none -> 36.4 us  [the longest x22 34.8 us: shifted(): return lax.ppermute(value, AXES, pairs)]
    dynamic_slice x39 -> x1, local copies, waits for them, and re-layouts: 29 us -> 0.01 us  [to_absolute(): lax.dynamic_slice_in_dim(jnp.concatenate([a, a], axis=1), (Z - z) % Z, Z,...]
    unnamed x14 -> x108, local copies, waits for them, and re-layouts: 4.27 us -> 33.2 us
    all_to_all x0 -> x1, blocking collectives: none -> 24.9 us  [local(): lax.all_to_all(jnp.broadcast_to(sent[None], (PEERS, *sent.shape)), 'dp',...]
    psum x1 -> x0, blocking collectives: 21.1 us -> none  [local(): lax.psum((weighted, mass, shift_sum, shift_count), 'dp')]
  transfers between devices with their start and end apart: 4 -> 26, of which waited for: 4 -> 10; matrix products, arithmetic and copies ran while one was open for 5% -> 5% of each run, Pallas kernels for 0% -> 5%
where the time goes in v1:
time: 184 us; the launch traced here: 181 us
  starting transfers between devices  41.7 us (23%)
  local copies, waits for them, and re-layouts  40.3 us (22%)
  waiting for transfers between devices  37.7 us (20%)
  blocking collectives  24.9 us (14%)
  Pallas kernels  20.1 us (11%)
  other arithmetic  14.6 us (8%)
    ppermute x22, starting transfers between devices, shifted(): return lax.ppermute(value, AXES, pairs)  34.8 us
    unnamed x108, local copies, waits for them, and re-layouts  33.2 us
    all_to_all x1, blocking collectives, local(): lax.all_to_all(jnp.broadcast_to(sent[None], (PEERS, *sent.shape)), 'dp',...  24.9 us
    all_to_all x1, waiting for transfers between devices, local(): lax.all_to_all(jnp.concatenate([packed, *lines], axis=1), 'dp', split_axi...  16.7 us
    ppermute x3, waiting for transfers between devices, z_partner(): return lax.ppermute(value, AXES, pairs)  11.8 us
    pallas_call x5, Pallas kernels, score_rows(): pl.pallas_call(functools.partial(score_kernel, len(rows)), out_shape=(jax...  11.3 us
    ppermute x22, waiting for transfers between devices, shifted(): return lax.ppermute(value, AXES, pairs)  9.19 us
    pallas_call x1, Pallas kernels, sum_rows(): pl.pallas_call(functools.partial(sum_kernel, [[r.shape[0] for r in group]...  8.8 us
  transfers between devices with their start and end apart: 26, of which 10 were waited for; matrix products, arithmetic and copies ran while one was open for 5% of the time, Pallas kernels for 5%

profile of v1, /device:TPU:1, one launch (start us, length us, event | category | flops | bytes accessed | tf_op | source)
XLA Modules:
  0.0 180.8 jit_solution(12980941137303472074)
XLA Ops:
  0.6 1.1 fusion.24
  1.7 3.6 %collective-permute-start.1 = (bf16[64,768]{1,0:T(8,128)(2,1)S(1)}, bf16[64,768]{1,0:T(8,128)(2,1)S(1)}, u32[]{:S(2)}, u32[]{:S(2)}) collective-permute-start(bf16[64,768]{1,0:T(8,128)(2,1)S(1)} %get-tuple-element.40), channel_id=1, source_target_pairs={{0,129},{8,137},{16,145},{24,153},{32,161},{40,169},{48,177},{56,1... | collective-permute-start | bytes 294920 | tf_op jit(solution)/shard_map/ppermute | solution.py:35
  6.3 1.6 multiply_reduce_fusion
  7.9 2.1 %collective-permute-done = bf16[64,768]{1,0:T(8,128)(2,1)S(1)} collective-permute-done((bf16[64,768]{1,0:T(8,128)(2,1)S(1)}, bf16[64,768]{1,0:T(8,128)(2,1)S(1)}, u32[]{:S(2)}, u32[]{:S(2)}) %collective-permute-start) | collective-permute-done | bytes 98336 | tf_op jit(solution)/shard_map/ppermute | solution.py:35
  10.1 5.7 %collective-permute-start.5 = (bf16[256,768]{1,0:T(8,128)(2,1)S(1)}, bf16[256,768]{1,0:T(8,128)(2,1)S(1)}, u32[]{:S(2)}, u32[]{:S(2)}) collective-permute-start(bf16[256,768]{1,0:T(8,128)(2,1)S(1)} %constant_dynamic-update-slice_fusion.refs_2_.refs_5_), channel_id=1, source_target_pairs={{0,112},{8,120},{16,0},{24,8},{32,16},{40,24},{48,32},{56,40},{64,... | collective-permute-start | bytes 1179656 | tf_op jit(solution)/shard_map/ppermute | solution.py:35
  15.7 1.3 convert_reduce_fusion
  17.7 4.3 %collective-permute-done.5.refs_4_.refs_9_ = bf16[256,768]{1,0:T(8,128)(2,1)S(1)} collective-permute-done((bf16[256,768]{1,0:T(8,128)(2,1)S(1)}, bf16[256,768]{1,0:T(8,128)(2,1)S(1)}, u32[]{:S(2)}, u32[]{:S(2)}) %collective-permute-start.5) | collective-permute-done | bytes 393248 | tf_op jit(solution)/shard_map/ppermute | solution.py:35
  22.0 3.4 %collective-permute-start.9 = (bf16[256,768]{1,0:T(8,128)(2,1)S(1)}, bf16[256,768]{1,0:T(8,128)(2,1)}, u32[]{:S(2)}, u32[]{:S(2)}) collective-permute-start(bf16[256,768]{1,0:T(8,128)(2,1)S(1)} %collective-permute-done.5.refs_4_.refs_9_), channel_id=1, source_target_pairs={{0,112},{8,120},{16,0},{24,8},{32,16},{40,24},{48,32},{56,40},{64,... | collective-permute-start | bytes 1179656 | tf_op jit(solution)/shard_map/ppermute | solution.py:35
  25.4 3.4 %collective-permute-start.2 = (bf16[256,768]{1,0:T(8,128)(2,1)S(1)}, bf16[256,768]{1,0:T(8,128)(2,1)S(1)}, u32[]{:S(2)}, u32[]{:S(2)}) collective-permute-start(bf16[256,768]{1,0:T(8,128)(2,1)S(1)} %constant_dynamic-update-slice_fusion.refs_2_.refs_5_), channel_id=1, source_target_pairs={{0,8},{8,0},{16,24},{24,16},{32,40},{40,32},{48,56},{56,48},{64,72... | collective-permute-start | bytes 1179656 | tf_op jit(solution)/shard_map/ppermute | solution.py:35
  30.8 3.5 %collective-permute-start.13 = (bf16[256,768]{1,0:T(8,128)(2,1)}, bf16[256,768]{1,0:T(8,128)(2,1)S(1)}, u32[]{:S(2)}, u32[]{:S(2)}) collective-permute-start(bf16[256,768]{1,0:T(8,128)(2,1)} %collective-permute-done.9.refs_4_.refs_13_), channel_id=1, source_target_pairs={{0,112},{8,120},{16,0},{24,8},{32,16},{40,24},{48,32},{56,40},{64,... | collective-permute-start | bytes 1179656 | tf_op jit(solution)/shard_map/ppermute | solution.py:35
  35.0 4.2 %collective-permute-start.10 = (bf16[256,768]{1,0:T(8,128)(2,1)}, bf16[256,768]{1,0:T(8,128)(2,1)}, u32[]{:S(2)}, u32[]{:S(2)}) collective-permute-start(bf16[256,768]{1,0:T(8,128)(2,1)} %collective-permute-done.9.refs_4_.refs_13_), channel_id=1, source_target_pairs={{0,8},{8,0},{16,24},{24,16},{32,40},{40,32},{48,56},{56,48},{64,72... | collective-permute-start | bytes 1179656 | tf_op jit(solution)/shard_map/ppermute | solution.py:35
  39.5 1.1 shard_map.59
  40.7 1.1 copy-done.21
  41.9 3.2 %shard_map.60 = (f32[768,1024]{1,0:T(8,128)S(1)}, f32[2,1024]{1,0:T(2,128)S(1)}) custom-call(bf16[768,768]{1,0:T(8,128)(2,1)S(1)} %copy-done, f32[768,1]{1,0:T(8,128)S(1)} %mul.145.refs_1_, bf16[256,768]{1,0:T(8,128)(2,1)} %collective-permute-done.3.refs_2_.refs_7_, bf16[256,768]{1,0:T(8,128)(2,1)} %collective-permute-done.4.refs_3_.refs_8_, ...), custom_call_target="tpu_custom_call" | custom-call | flops 1207959552 | bytes 4325376 | tf_op jit(solution)/shard_map/pallas_call | solution.py:66
  45.1 1.6 copy-done.33
  46.8 3.0 %collective-permute-start.17 = (bf16[128,768]{1,0:T(8,128)(2,1)S(1)}, bf16[128,768]{1,0:T(8,128)(2,1)S(1)}, u32[]{:S(2)}, u32[]{:S(2)}) collective-permute-start(bf16[128,768]{1,0:T(8,128)(2,1)S(1)} %slice.312), channel_id=1, source_target_pairs={{0,112},{8,120},{16,0},{24,8},{32,16},{40,24},{48,32},{56,40},{64,... | collective-permute-start | bytes 589832 | tf_op jit(solution)/shard_map/ppermute | solution.py:35
  50.6 3.3 %shard_map.61 = (f32[768,1024]{1,0:T(8,128)S(1)}, f32[2,1024]{1,0:T(2,128)S(1)}) custom-call(bf16[768,768]{1,0:T(8,128)(2,1)S(1)} %copy-done, f32[768,1]{1,0:T(8,128)S(1)} %mul.145.refs_1_, bf16[256,768]{1,0:T(8,128)(2,1)} %collective-permute-done.7.refs_2_.refs_11_, bf16[256,768]{1,0:T(8,128)(2,1)} %collective-permute-done.8.refs_3_.refs_12_, ...), custom_call_target="tpu_custom_call" | custom-call | flops 1207959552 | bytes 4325376 | tf_op jit(solution)/shard_map/pallas_call | solution.py:66
  53.9 1.7 copy-done.35
  56.8 1.6 collective-permute-start.16
  60.2 1.6 shard_map.63
  62.5 1.1 copy-done.23
  64.3 2.0 %shard_map.62 = (f32[768,1024]{1,0:T(8,128)S(1)}, f32[2,1024]{1,0:T(2,128)S(1)}) custom-call(bf16[768,768]{1,0:T(8,128)(2,1)S(1)} %copy-done, f32[768,1]{1,0:T(8,128)S(1)} %mul.145.refs_1_, bf16[256,768]{1,0:T(8,128)(2,1)S(1)} %collective-permute-done.11.refs_2_.refs_15_, bf16[256,768]{1,0:T(8,128)(2,1)S(1)} %collective-permute-done.12.refs_3_.refs_16_, ...), custom_call_target="tpu_custom_call" | custom-call | flops 1207959552 | bytes 4325376 | tf_op jit(solution)/shard_map/pallas_call | solution.py:66
  66.3 1.7 copy-done.37
  68.1 1.5 concatenate.52
  71.2 2.7 %collective-permute-start.19 = (f32[3,8,2,128]{3,1,2,0:T(8,128)S(1)}, f32[3,8,2,128]{3,1,2,0:T(8,128)S(1)}, u32[]{:S(2)}, u32[]{:S(2)}) collective-permute-start(f32[3,8,2,128]{3,1,2,0:T(8,128)S(1)} %get-tuple-element.50), channel_id=1, source_target_pairs={{0,129},{8,137},{16,145},{24,153},{32,161},{40,169},{48,177},{56,1... | collective-permute-start | bytes 73736 | tf_op jit(solution)/shard_map/ppermute | solution.py:35
  73.9 1.2 collective-permute-done.20
  76.1 1.3 collective-permute-start.21
  78.4 2.9 %collective-permute-done.22 = f32[3,8,2,256]{3,1,2,0:T(8,128)S(1)} collective-permute-done((f32[3,8,2,256]{3,1,2,0:T(8,128)S(1)}, f32[3,8,2,256]{3,1,2,0:T(8,128)S(1)}, u32[]{:S(2)}, u32[]{:S(2)}) %collective-permute-start.22) | collective-permute-done | bytes 49184 | tf_op jit(solution)/shard_map/ppermute | solution.py:40
  81.5 4.1 %collective-permute-done.23 = f32[3,8,2,256]{3,1,2,0:T(8,128)S(1)} collective-permute-done((f32[3,8,2,256]{3,1,2,0:T(8,128)S(1)}, f32[3,8,2,256]{3,1,2,0:T(8,128)S(1)}, u32[]{:S(2)}, u32[]{:S(2)}) %collective-permute-start.23) | collective-permute-done | bytes 49184 | tf_op jit(solution)/shard_map/ppermute | solution.py:40
  85.6 1.4 collective-permute-start.24
  87.7 4.8 %collective-permute-done.24 = f32[3,8,2,256]{3,1,2,0:T(8,128)S(1)} collective-permute-done((f32[3,8,2,256]{3,1,2,0:T(8,128)S(1)}, f32[3,8,2,256]{3,1,2,0:T(8,128)S(1)}, u32[]{:S(2)}, u32[]{:S(2)}) %collective-permute-start.24) | collective-permute-done | bytes 49184 | tf_op jit(solution)/shard_map/ppermute | solution.py:40
  93.4 1.0 copy-done.2
  94.4 1.0 copy-done.6
  100.1 1.0 copy-done.19
  101.1 1.4 copy-done.22
  102.5 1.4 copy-done.24
  103.9 1.0 copy-done.26
  107.6 1.9 %copy-done.34 = f32[768,1024]{1,0:T(8,128)S(1)} copy-done((f32[768,1024]{1,0:T(8,128)S(1)}, f32[768,1024]{1,0:T(8,128)}, u32[]{:S(2)}) %copy-start.34) | copy-done | bytes 3145752
  109.5 1.9 %copy-done.36 = f32[768,1024]{1,0:T(8,128)S(1)} copy-done((f32[768,1024]{1,0:T(8,128)S(1)}, f32[768,1024]{1,0:T(8,128)}, u32[]{:S(2)}) %copy-start.36) | copy-done | bytes 3145752
  111.4 1.9 %copy-done.38 = f32[768,1024]{1,0:T(8,128)S(1)} copy-done((f32[768,1024]{1,0:T(8,128)S(1)}, f32[768,1024]{1,0:T(8,128)}, u32[]{:S(2)}) %copy-start.38) | copy-done | bytes 3145752
  113.3 8.8 %shard_map.64 = (f32[768,768]{1,0:T(8,128)S(1)}, f32[768,1]{1,0:T(8,128)S(1)}, f32[64,768]{1,0:T(8,128)S(1)}, f32[64,1]{1,0:T(8,128)S(1)}) custom-call(f32[768,512]{1,0:T(8,128)S(1)} %copy-done.22, f32[768,1024]{1,0:T(8,128)S(1)} %copy-done.34, f32[768,1024]{1,0:T(8,128)S(1)} %copy-done.36, f32[768,1024]{1,0:T(8,128)S(1)} %copy-done.38, ...), custom_call_target="tpu_custom_call" | custom-call | flops 5234491392 | bytes 18874368 | tf_op jit(solution)/shard_map/pallas_call | solution.py:125
  125.0 1.2 reduce.1
  126.3 1.3 abs_reduce_fusion
  128.1 1.7 pad_maximum_fusion.1
  129.8 5.4 %all-to-all-start = ((f16[8,107,768]{2,1,0:T(8,128)(2,1)}), f16[8,107,768]{2,1,0:T(8,128)(2,1)S(1)}, u32[]{:S(2)}, u32[]{:S(2)}) async-start(f16[8,107,768]{2,1,0:T(8,128)(2,1)} %pad_maximum_fusion.1), calls=%async_computation | async-start | bytes 2752512 | tf_op jit(solution)/shard_map/all_to_all | solution.py:247
  135.2 16.7 %all-to-all-done = f16[8,107,768]{2,1,0:T(8,128)(2,1)S(1)} async-done(((f16[8,107,768]{2,1,0:T(8,128)(2,1)}), f16[8,107,768]{2,1,0:T(8,128)(2,1)S(1)}, u32[]{:S(2)}, u32[]{:S(2)}) %all-to-all-start) | async-done | bytes 1314848 | tf_op jit(solution)/shard_map/all_to_all | solution.py:247
  153.1 24.9 %all_to_all.10 = f16[8,105,768]{2,1,0:T(8,128)(2,1)S(1)} all-to-all(f16[8,105,768]{2,1,0:T(8,128)(2,1)S(1)} %broadcast_in_dim.48), channel_id=1, replica_groups=mesh['blk'=32,'dp'=8] {'dp'}, dimensions={0} | all-to-all | bytes 2580480 | tf_op jit(solution)/shard_map/all_to_all | solution.py:262
  179.2 1.6 slice.376
  (207 shorter events, 28.1 us)
Async XLA Ops:
  0.6 38.9 %copy-start = (bf16[768,768]{1,0:T(8,128)(2,1)S(1)}, bf16[768,768]{1,0:T(8,128)(2,1)}, u32[]{:S(2)}) copy-start(bf16[768,768]{1,0:T(8,128)(2,1)} %refs_0_.9) | copy-start | bytes 3538948
  1.7 8.3 %collective-permute-start.1 = (bf16[64,768]{1,0:T(8,128)(2,1)S(1)}, bf16[64,768]{1,0:T(8,128)(2,1)S(1)}, u32[]{:S(2)}, u32[]{:S(2)}) collective-permute-start(bf16[64,768]{1,0:T(8,128)(2,1)S(1)} %get-tuple-element.40), channel_id=1, source_target_pairs={{0,129},{8,137},{16,145},{24,153},{32,161},{40,169},{48,177},{56,1... | collective-permute-start | bytes 294920 | tf_op jit(solution)/shard_map/ppermute | solution.py:35
  5.3 4.7 %collective-permute-start = (bf16[64,768]{1,0:T(8,128)(2,1)S(1)}, bf16[64,768]{1,0:T(8,128)(2,1)S(1)}, u32[]{:S(2)}, u32[]{:S(2)}) collective-permute-start(bf16[64,768]{1,0:T(8,128)(2,1)S(1)} %get-tuple-element.41), channel_id=1, source_target_pairs={{0,128},{8,136},{16,144},{24,152},{32,160},{40,168},{48,176},{56,1... | collective-permute-start | bytes 294920 | tf_op jit(solution)/shard_map/ppermute | solution.py:35
  10.1 35.0 %copy-start.1 = (bf16[256,768]{1,0:T(8,128)(2,1)}, bf16[256,768]{1,0:T(8,128)(2,1)S(1)}, u32[]{:S(2)}) copy-start(bf16[256,768]{1,0:T(8,128)(2,1)S(1)} %constant_dynamic-update-slice_fusion.refs_2_.refs_5_) | copy-start | bytes 1179652
  10.1 12.0 %collective-permute-start.5 = (bf16[256,768]{1,0:T(8,128)(2,1)S(1)}, bf16[256,768]{1,0:T(8,128)(2,1)S(1)}, u32[]{:S(2)}, u32[]{:S(2)}) collective-permute-start(bf16[256,768]{1,0:T(8,128)(2,1)S(1)} %constant_dynamic-update-slice_fusion.refs_2_.refs_5_), channel_id=1, source_target_pairs={{0,112},{8,120},{16,0},{24,8},{32,16},{40,24},{48,32},{56,40},{64,... | collective-permute-start | bytes 1179656 | tf_op jit(solution)/shard_map/ppermute | solution.py:35
  15.7 9.7 %collective-permute-start.3 = (bf16[256,768]{1,0:T(8,128)(2,1)S(1)}, bf16[256,768]{1,0:T(8,128)(2,1)}, u32[]{:S(2)}, u32[]{:S(2)}) collective-permute-start(bf16[256,768]{1,0:T(8,128)(2,1)S(1)} %constant_dynamic-update-slice_fusion.refs_2_.refs_5_), channel_id=1, source_target_pairs={{0,16},{8,24},{16,32},{24,40},{32,48},{40,56},{48,64},{56,72},{64,... | collective-permute-start | bytes 1179656 | tf_op jit(solution)/shard_map/ppermute | solution.py:35
  22.0 23.1 %copy-start.25 = (bf16[256,768]{1,0:T(8,128)(2,1)}, bf16[256,768]{1,0:T(8,128)(2,1)S(1)}, u32[]{:S(2)}) copy-start(bf16[256,768]{1,0:T(8,128)(2,1)S(1)} %collective-permute-done.5.refs_4_.refs_9_) | copy-start | bytes 1179652
  22.0 8.8 %collective-permute-start.9 = (bf16[256,768]{1,0:T(8,128)(2,1)S(1)}, bf16[256,768]{1,0:T(8,128)(2,1)}, u32[]{:S(2)}, u32[]{:S(2)}) collective-permute-start(bf16[256,768]{1,0:T(8,128)(2,1)S(1)} %collective-permute-done.5.refs_4_.refs_9_), channel_id=1, source_target_pairs={{0,112},{8,120},{16,0},{24,8},{32,16},{40,24},{48,32},{56,40},{64,... | collective-permute-start | bytes 1179656 | tf_op jit(solution)/shard_map/ppermute | solution.py:35
  25.4 8.9 %collective-permute-start.7 = (bf16[256,768]{1,0:T(8,128)(2,1)}, bf16[256,768]{1,0:T(8,128)(2,1)}, u32[]{:S(2)}, u32[]{:S(2)}) collective-permute-start(bf16[256,768]{1,0:T(8,128)(2,1)} %collective-permute-done.3.refs_2_.refs_7_), channel_id=1, source_target_pairs={{0,16},{8,24},{16,32},{24,40},{32,48},{40,56},{48,64},{56,72},{64,... | collective-permute-start | bytes 1179656 | tf_op jit(solution)/shard_map/ppermute | solution.py:35
  25.4 9.6 %collective-permute-start.2 = (bf16[256,768]{1,0:T(8,128)(2,1)S(1)}, bf16[256,768]{1,0:T(8,128)(2,1)S(1)}, u32[]{:S(2)}, u32[]{:S(2)}) collective-permute-start(bf16[256,768]{1,0:T(8,128)(2,1)S(1)} %constant_dynamic-update-slice_fusion.refs_2_.refs_5_), channel_id=1, source_target_pairs={{0,8},{8,0},{16,24},{24,16},{32,40},{40,32},{48,56},{56,48},{64,72... | collective-permute-start | bytes 1179656 | tf_op jit(solution)/shard_map/ppermute | solution.py:35
  28.8 10.4 %collective-permute-start.6 = (bf16[256,768]{1,0:T(8,128)(2,1)S(1)}, bf16[256,768]{1,0:T(8,128)(2,1)}, u32[]{:S(2)}, u32[]{:S(2)}) collective-permute-start(bf16[256,768]{1,0:T(8,128)(2,1)S(1)} %collective-permute-done.5.refs_4_.refs_9_), channel_id=1, source_target_pairs={{0,8},{8,0},{16,24},{24,16},{32,40},{40,32},{48,56},{56,48},{64,72... | collective-permute-start | bytes 1179656 | tf_op jit(solution)/shard_map/ppermute | solution.py:35
  29.0 10.2 %copy-start.40 = (pred[8,2]{0,1:T(4,128)(4,1)}, pred[8,2]{0,1:T(4,128)(4,1)S(1)}, u32[]{:S(2)}) copy-start(pred[8,2]{0,1:T(4,128)(4,1)S(1)} %broadcast_and_fusion) | copy-start | bytes 52
  29.0 12.8 %collective-permute-start.4 = (bf16[256,768]{1,0:T(8,128)(2,1)}, bf16[256,768]{1,0:T(8,128)(2,1)}, u32[]{:S(2)}, u32[]{:S(2)}) collective-permute-start(bf16[256,768]{1,0:T(8,128)(2,1)} %collective-permute-done.3.refs_2_.refs_7_), channel_id=1, source_target_pairs={{0,8},{8,0},{16,24},{24,16},{32,40},{40,32},{48,56},{56,48},{64,72... | collective-permute-start | bytes 1179656 | tf_op jit(solution)/shard_map/ppermute | solution.py:35
  30.5 8.7 %copy-start.39 = (f32[256]{0:T(256)}, f32[256]{0:T(256)S(1)}, u32[]{:S(2)}) copy-start(f32[256]{0:T(256)S(1)} %pad.22) | copy-start | bytes 3076
  30.8 15.9 %collective-permute-start.13 = (bf16[256,768]{1,0:T(8,128)(2,1)}, bf16[256,768]{1,0:T(8,128)(2,1)S(1)}, u32[]{:S(2)}, u32[]{:S(2)}) collective-permute-start(bf16[256,768]{1,0:T(8,128)(2,1)} %collective-permute-done.9.refs_4_.refs_13_), channel_id=1, source_target_pairs={{0,112},{8,120},{16,0},{24,8},{32,16},{40,24},{48,32},{56,40},{64,... | collective-permute-start | bytes 1179656 | tf_op jit(solution)/shard_map/ppermute | solution.py:35
  34.3 15.5 %collective-permute-start.11 = (bf16[256,768]{1,0:T(8,128)(2,1)}, bf16[256,768]{1,0:T(8,128)(2,1)S(1)}, u32[]{:S(2)}, u32[]{:S(2)}) collective-permute-start(bf16[256,768]{1,0:T(8,128)(2,1)} %collective-permute-done.7.refs_2_.refs_11_), channel_id=1, source_target_pairs={{0,16},{8,24},{16,32},{24,40},{32,48},{40,56},{48,64},{56,72},{64,... | collective-permute-start | bytes 1179656 | tf_op jit(solution)/shard_map/ppermute | solution.py:35
  35.0 10.1 %copy-start.5 = (bf16[256,768]{1,0:T(8,128)(2,1)}, bf16[256,768]{1,0:T(8,128)(2,1)S(1)}, u32[]{:S(2)}) copy-start(bf16[256,768]{1,0:T(8,128)(2,1)S(1)} %collective-permute-done.2.refs_3_.refs_6_) | copy-start | bytes 1179652
  35.0 15.5 %collective-permute-start.10 = (bf16[256,768]{1,0:T(8,128)(2,1)}, bf16[256,768]{1,0:T(8,128)(2,1)}, u32[]{:S(2)}, u32[]{:S(2)}) collective-permute-start(bf16[256,768]{1,0:T(8,128)(2,1)} %collective-permute-done.9.refs_4_.refs_13_), channel_id=1, source_target_pairs={{0,8},{8,0},{16,24},{24,16},{32,40},{40,32},{48,56},{56,48},{64,72... | collective-permute-start | bytes 1179656 | tf_op jit(solution)/shard_map/ppermute | solution.py:35
  39.3 11.3 %collective-permute-start.8 = (bf16[256,768]{1,0:T(8,128)(2,1)}, bf16[256,768]{1,0:T(8,128)(2,1)}, u32[]{:S(2)}, u32[]{:S(2)}) collective-permute-start(bf16[256,768]{1,0:T(8,128)(2,1)} %collective-permute-done.7.refs_2_.refs_11_), channel_id=1, source_target_pairs={{0,8},{8,0},{16,24},{24,16},{32,40},{40,32},{48,56},{56,48},{64,72... | collective-permute-start | bytes 1179656 | tf_op jit(solution)/shard_map/ppermute | solution.py:35
  45.1 1.6 copy-start.33
  46.8 17.5 %copy-start.16 = (bf16[256,768]{1,0:T(8,128)(2,1)}, bf16[256,768]{1,0:T(8,128)(2,1)S(1)}, u32[]{:S(2)}) copy-start(bf16[256,768]{1,0:T(8,128)(2,1)S(1)} %collective-permute-done.13.refs_4_.refs_17_) | copy-start | bytes 1179652
  46.8 8.8 %collective-permute-start.17 = (bf16[128,768]{1,0:T(8,128)(2,1)S(1)}, bf16[128,768]{1,0:T(8,128)(2,1)S(1)}, u32[]{:S(2)}, u32[]{:S(2)}) collective-permute-start(bf16[128,768]{1,0:T(8,128)(2,1)S(1)} %slice.312), channel_id=1, source_target_pairs={{0,112},{8,120},{16,0},{24,8},{32,16},{40,24},{48,32},{56,40},{64,... | collective-permute-start | bytes 589832 | tf_op jit(solution)/shard_map/ppermute | solution.py:35
  49.8 14.5 %copy-start.18 = (bf16[256,768]{1,0:T(8,128)(2,1)}, bf16[256,768]{1,0:T(8,128)(2,1)S(1)}, u32[]{:S(2)}) copy-start(bf16[256,768]{1,0:T(8,128)(2,1)S(1)} %collective-permute-done.11.refs_2_.refs_15_) | copy-start | bytes 1179652
  49.8 7.0 %collective-permute-start.15 = (bf16[128,768]{1,0:T(8,128)(2,1)S(1)}, bf16[128,768]{1,0:T(8,128)(2,1)S(1)}, u32[]{:S(2)}, u32[]{:S(2)}) collective-permute-start(bf16[128,768]{1,0:T(8,128)(2,1)S(1)} %slice.311), channel_id=1, source_target_pairs={{0,16},{8,24},{16,32},{24,40},{32,48},{40,56},{48,64},{56,72},{64,... | collective-permute-start | bytes 589832 | tf_op jit(solution)/shard_map/ppermute | solution.py:35
  53.9 1.7 copy-start.35
  55.6 10.7 %copy-start.8 = (bf16[128,768]{1,0:T(8,128)(2,1)}, bf16[128,768]{1,0:T(8,128)(2,1)S(1)}, u32[]{:S(2)}) copy-start(bf16[128,768]{1,0:T(8,128)(2,1)S(1)} %collective-permute-done.17.refs_4_.refs_21_) | copy-start | bytes 589828
  55.6 4.6 %collective-permute-start.18 = (bf16[128,768]{1,0:T(8,128)(2,1)S(1)}, bf16[128,768]{1,0:T(8,128)(2,1)S(1)}, u32[]{:S(2)}, u32[]{:S(2)}) collective-permute-start(bf16[128,768]{1,0:T(8,128)(2,1)S(1)} %collective-permute-done.17.refs_4_.refs_21_), channel_id=1, source_target_pairs={{0,8},{8,0},{16,24},{24,16},{32,40},{40,32},{48,56},{56,48},{64,72... | collective-permute-start | bytes 589832 | tf_op jit(solution)/shard_map/ppermute | solution.py:35
  56.8 9.5 %copy-start.10 = (bf16[128,768]{1,0:T(8,128)(2,1)}, bf16[128,768]{1,0:T(8,128)(2,1)S(1)}, u32[]{:S(2)}) copy-start(bf16[128,768]{1,0:T(8,128)(2,1)S(1)} %collective-permute-done.15.refs_2_.refs_19_) | copy-start | bytes 589828
  56.8 3.4 %collective-permute-start.16 = (bf16[128,768]{1,0:T(8,128)(2,1)S(1)}, bf16[128,768]{1,0:T(8,128)(2,1)S(1)}, u32[]{:S(2)}, u32[]{:S(2)}) collective-permute-start(bf16[128,768]{1,0:T(8,128)(2,1)S(1)} %collective-permute-done.15.refs_2_.refs_19_), channel_id=1, source_target_pairs={{0,8},{8,0},{16,24},{24,16},{32,40},{40,32},{48,56},{56,48},{64,72... | collective-permute-start | bytes 589832 | tf_op jit(solution)/shard_map/ppermute | solution.py:35
  59.7 4.6 %collective-permute-start.14 = (bf16[256,768]{1,0:T(8,128)(2,1)S(1)}, bf16[256,768]{1,0:T(8,128)(2,1)S(1)}, u32[]{:S(2)}, u32[]{:S(2)}) collective-permute-start(bf16[256,768]{1,0:T(8,128)(2,1)S(1)} %collective-permute-done.13.refs_4_.refs_17_), channel_id=1, source_target_pairs={{0,8},{8,0},{16,24},{24,16},{32,40},{40,32},{48,56},{56,48},{64,72... | collective-permute-start | bytes 1179656 | tf_op jit(solution)/shard_map/ppermute | solution.py:35
  59.7 4.6 %collective-permute-start.12 = (bf16[256,768]{1,0:T(8,128)(2,1)S(1)}, bf16[256,768]{1,0:T(8,128)(2,1)S(1)}, u32[]{:S(2)}, u32[]{:S(2)}) collective-permute-start(bf16[256,768]{1,0:T(8,128)(2,1)S(1)} %collective-permute-done.11.refs_2_.refs_15_), channel_id=1, source_target_pairs={{0,8},{8,0},{16,24},{24,16},{32,40},{40,32},{48,56},{56,48},{64,72... | collective-permute-start | bytes 1179656 | tf_op jit(solution)/shard_map/ppermute | solution.py:35
  60.2 1.6 copy-start.14
  64.3 11.0 %copy-start.27 = (bf16[256,768]{1,0:T(8,128)(2,1)}, bf16[256,768]{1,0:T(8,128)(2,1)S(1)}, u32[]{:S(2)}) copy-start(bf16[256,768]{1,0:T(8,128)(2,1)S(1)} %collective-permute-done.14.refs_5_.refs_18_) | copy-start | bytes 1179652
  64.3 11.0 %copy-start.29 = (bf16[256,768]{1,0:T(8,128)(2,1)}, bf16[256,768]{1,0:T(8,128)(2,1)S(1)}, u32[]{:S(2)}) copy-start(bf16[256,768]{1,0:T(8,128)(2,1)S(1)} %collective-permute-done.12.refs_3_.refs_16_) | copy-start | bytes 1179652
  66.3 1.7 copy-start.37
  71.2 3.9 %collective-permute-start.20 = (f32[3,8,2,128]{3,1,2,0:T(8,128)S(1)}, f32[3,8,2,128]{3,1,2,0:T(8,128)S(1)}, u32[]{:S(2)}, u32[]{:S(2)}) collective-permute-start(f32[3,8,2,128]{3,1,2,0:T(8,128)S(1)} %get-tuple-element.49), channel_id=1, source_target_pairs={{0,128},{8,136},{16,144},{24,152},{32,160},{40,168},{48,176},{56,1... | collective-permute-start | bytes 73736 | tf_op jit(solution)/shard_map/ppermute | solution.py:35
  71.2 4.0 %collective-permute-start.19 = (f32[3,8,2,128]{3,1,2,0:T(8,128)S(1)}, f32[3,8,2,128]{3,1,2,0:T(8,128)S(1)}, u32[]{:S(2)}, u32[]{:S(2)}) collective-permute-start(f32[3,8,2,128]{3,1,2,0:T(8,128)S(1)} %get-tuple-element.50), channel_id=1, source_target_pairs={{0,129},{8,137},{16,145},{24,153},{32,161},{40,169},{48,177},{56,1... | collective-permute-start | bytes 73736 | tf_op jit(solution)/shard_map/ppermute | solution.py:35
  76.1 2.2 %collective-permute-start.21 = (f32[3,8,2,256]{3,1,2,0:T(8,128)S(1)}, f32[3,8,2,256]{3,1,2,0:T(8,128)S(1)}, u32[]{:S(2)}, u32[]{:S(2)}) collective-permute-start(f32[3,8,2,256]{3,1,2,0:T(8,128)S(1)} %pad_maximum_fusion.5), channel_id=1, source_target_pairs={{0,8},{8,0},{16,24},{24,16},{32,40},{40,32},{48,56},{56,48},{64,72... | collective-permute-start | bytes 147464 | tf_op jit(solution)/shard_map/ppermute | solution.py:35
  78.3 3.0 %collective-permute-start.22 = (f32[3,8,2,256]{3,1,2,0:T(8,128)S(1)}, f32[3,8,2,256]{3,1,2,0:T(8,128)S(1)}, u32[]{:S(2)}, u32[]{:S(2)}) collective-permute-start(f32[3,8,2,256]{3,1,2,0:T(8,128)S(1)} %pad_maximum_fusion.6), channel_id=1, source_target_pairs={{0,16},{8,24},{16,0},{24,8},{32,48},{40,56},{48,32},{56,40},{64,80... | collective-permute-start | bytes 147464 | tf_op jit(solution)/shard_map/ppermute | solution.py:40
  81.4 4.2 %collective-permute-start.23 = (f32[3,8,2,256]{3,1,2,0:T(8,128)S(1)}, f32[3,8,2,256]{3,1,2,0:T(8,128)S(1)}, u32[]{:S(2)}, u32[]{:S(2)}) collective-permute-start(f32[3,8,2,256]{3,1,2,0:T(8,128)S(1)} %pad_maximum_fusion.7), channel_id=1, source_target_pairs={{0,32},{8,40},{16,48},{24,56},{32,0},{40,8},{48,16},{56,24},{64,96... | collective-permute-start | bytes 147464 | tf_op jit(solution)/shard_map/ppermute | solution.py:40
  85.6 6.9 %collective-permute-start.24 = (f32[3,8,2,256]{3,1,2,0:T(8,128)S(1)}, f32[3,8,2,256]{3,1,2,0:T(8,128)S(1)}, u32[]{:S(2)}, u32[]{:S(2)}) collective-permute-start(f32[3,8,2,256]{3,1,2,0:T(8,128)S(1)} %pad_maximum_fusion.8), channel_id=1, source_target_pairs={{0,64},{8,72},{16,80},{24,88},{32,96},{40,104},{48,112},{56,120},{... | collective-permute-start | bytes 147464 | tf_op jit(solution)/shard_map/ppermute | solution.py:40
  101.1 1.4 copy-start.22
  102.5 1.4 copy-start.24
  107.6 1.9 %copy-start.34 = (f32[768,1024]{1,0:T(8,128)S(1)}, f32[768,1024]{1,0:T(8,128)}, u32[]{:S(2)}) copy-start(f32[768,1024]{1,0:T(8,128)} %copy-done.33) | copy-start | bytes 9437188
  109.5 1.9 %copy-start.36 = (f32[768,1024]{1,0:T(8,128)S(1)}, f32[768,1024]{1,0:T(8,128)}, u32[]{:S(2)}) copy-start(f32[768,1024]{1,0:T(8,128)} %copy-done.35) | copy-start | bytes 9437188
  111.4 1.9 %copy-start.38 = (f32[768,1024]{1,0:T(8,128)S(1)}, f32[768,1024]{1,0:T(8,128)}, u32[]{:S(2)}) copy-start(f32[768,1024]{1,0:T(8,128)} %copy-done.37) | copy-start | bytes 9437188
  126.3 1.3 copy-start.4
  129.8 22.0 %all-to-all-start = ((f16[8,107,768]{2,1,0:T(8,128)(2,1)}), f16[8,107,768]{2,1,0:T(8,128)(2,1)S(1)}, u32[]{:S(2)}, u32[]{:S(2)}) async-start(f16[8,107,768]{2,1,0:T(8,128)(2,1)} %pad_maximum_fusion.1), calls=%async_computation | async-start | bytes 2752512 | tf_op jit(solution)/shard_map/all_to_all | solution.py:247
  (19 other events, 17.0 us)

commit v2 on v1

v2 whole, which is shorter than its diff:
```python
import functools
import math

import jax
import jax.numpy as jnp
from jax import lax
from jax.experimental import pallas as pl
from jax.experimental.pallas import tpu as pltpu
from jax.sharding import PartitionSpec as P

SLOTS = 64
X, Y, Z, C = 4, 4, 8, 2
PEERS = X * Y // 2
AXES = ("blk", "dp")
PRIOR = 0.5
MIB = 1 << 20
LANES = 128
TILE = 256


def place(x, y, z, c):
    return ((y % 2 * Z + z) * C + c) * PEERS + x * 2 + y // 2


def chips():
    for x in range(X):
        for y in range(Y):
            for z in range(Z):
                for c in range(C):
                    yield x, y, z, c


def shifted(value, dy=0, dz=0, dc=0):
    pairs = [
        (place(x, y, z, c), place(x, (y + dy) % Y, (z + dz) % Z, (c + dc) % C)) for x, y, z, c in chips()
    ]
    return lax.ppermute(value, AXES, pairs)


def lower_half():
    return lax.broadcasted_iota(jnp.int32, (Z, LANES), 1) < LANES // 2


def score_kernel(plan, count, *refs):
    books, norms, sources = refs[:2], refs[2:4], refs[4 : 4 + count]
    expos, rows, stats = refs[4 + count : 6 + count], refs[6 + count], refs[7 + count]
    k, width = books[0].shape
    n = rows.shape[0]
    for s, a, m, b in plan:
        rows[b : b + m, :] = sources[s][a : a + m, :]
    factor = 2.0 / math.sqrt(width)
    for at in range(0, n, TILE):
        m = min(TILE, n - at)
        block = rows[at : at + m, :]
        scores = [
            (
                lax.dot_general(
                    book[...], block, (((1,), (1,)), ((), ())), preferred_element_type=jnp.float32
                )
                - norm[...]
            )
            * factor
            for book, norm in zip(books, norms)
        ]
        top = jnp.maximum(*(jnp.max(part, axis=0, keepdims=True) for part in scores))
        total = jnp.zeros((1, m), jnp.float32)
        for part, expo in zip(scores, expos):
            value = jnp.exp(part - top)
            total += jnp.sum(value, axis=0, keepdims=True)
            expo[:, at : at + m] = value.astype(jnp.bfloat16)
        for j in range(0, m, LANES):
            g = (at + j) // LANES
            stats[0, g : g + 1, :] = top[:, j : j + LANES]
            stats[1, g : g + 1, :] = total[:, j : j + LANES]


def score_rows(books, norms, sources, plan):
    k, width = books[0].shape
    n = sum(p[2] for p in plan)
    whole = pl.BlockSpec(memory_space=pltpu.VMEM)
    return pl.pallas_call(
        functools.partial(score_kernel, plan, len(sources)),
        in_specs=[whole] * (4 + len(sources)),
        out_specs=(whole,) * 4,
        out_shape=(
            jax.ShapeDtypeStruct((k, n), jnp.bfloat16),
            jax.ShapeDtypeStruct((k, n), jnp.bfloat16),
            jax.ShapeDtypeStruct((n, width), jnp.bfloat16),
            jax.ShapeDtypeStruct((2, n // LANES, LANES), jnp.float32),
        ),
        compiler_params=pltpu.CompilerParams(vmem_limit_bytes=20 * MIB),
        cost_estimate=pl.CostEstimate(
            flops=4 * k * width * n, bytes_accessed=4 * k * width + 4 * k * n, transcendentals=2 * k * n
        ),
    )(*books, *norms, *sources)


def arrange_kernel(groups, position, slots, *refs):
    stats, (out, near, far) = refs[:-3], refs[-3:]
    z = position[0]
    out[2] = jnp.zeros((2, Z, LANES), jnp.float32)
    for which in range(2):
        g = 0
        for stage in stats:
            for i in range(stage.shape[1]):
                side, off = groups[g]
                at = lax.rem(z + off, Z)
                (near, far)[side][pl.ds(at, 1), :] = stage[which, i : i + 1, :]
                g += 1
        out[which, 0] = jnp.where(lower_half(), near[...], far[...])
        out[which, 1] = jnp.where(lower_half(), far[...], near[...])
    first = lax.broadcasted_iota(jnp.int32, (1, LANES), 1) < LANES // 2
    out[2, 0, pl.ds(z, 1), :] = jnp.where(first, slots[...], 0.0)
    out[2, 1, pl.ds(z, 1), :] = jnp.where(first, 0.0, slots[...])


def arrange(groups, position, slots, stats):
    return pl.pallas_call(
        functools.partial(arrange_kernel, groups),
        in_specs=[pl.BlockSpec(memory_space=pltpu.SMEM)]
        + [pl.BlockSpec(memory_space=pltpu.VMEM)] * (1 + len(stats)),
        out_specs=pl.BlockSpec(memory_space=pltpu.VMEM),
        out_shape=jax.ShapeDtypeStruct((3, 2, Z, LANES), jnp.float32),
        scratch_shapes=[pltpu.VMEM((Z, LANES), jnp.float32)] * 2,
        compiler_params=pltpu.CompilerParams(vmem_limit_bytes=4 * MIB),
    )(position, slots, *stats)


def sum_kernel(groups, sizes, position, near, parts, *refs):
    stages = len(sizes)
    expo_in, rows_in = refs[:stages], refs[stages : 2 * stages]
    sums, counts = refs[2 * stages : 2 * stages + 2]
    weights, rows, scale, slot = refs[2 * stages + 2 :]
    k, width = expo_in[0].shape[0], rows.shape[1]
    n = rows.shape[0]
    part, each = k // PEERS, SLOTS // PEERS
    z, first_slot = position[0], position[1]

    def unfolded(pair):
        return jnp.where(lower_half(), pair[0], pair[1]), jnp.where(lower_half(), pair[1], pair[0])

    ratio, number = [], []
    for i in range(2):
        top = functools.reduce(jnp.maximum, [parts[j, 0, i] for j in range(Z)])
        whole = sum(parts[j, 1, i] * jnp.exp(parts[j, 0, i] - top) for j in range(Z))
        ratio.append(jnp.exp(near[0, i] - top) / whole)
        number.append(sum(parts[j, 2, i] for j in range(Z)))
    scale[0], scale[1] = unfolded(ratio)
    slot[0], slot[1] = unfolded(number)

    def line(ref, g):
        side, off = groups[g]
        return ref[side, pl.ds(lax.rem(z + off, Z), 1), :]

    heavy = jnp.zeros((k, LANES), jnp.float32)
    hits = jnp.zeros((LANES, LANES), jnp.float32)
    want = lax.broadcasted_iota(jnp.int32, (LANES, LANES), 0) + first_slot
    total = None
    at, g, done = 0, 0, 0
    for s in range(stages):
        rows[at : at + sizes[s], :] = rows_in[s][...]
        for j in range(0, sizes[s], LANES):
            w = (expo_in[s][:, j : j + LANES].astype(jnp.float32) * line(scale, g)).astype(jnp.bfloat16)
            heavy += w.astype(jnp.float32)
            weights[:k, at + j : at + j + LANES] = w
            hot = jnp.where(want == line(slot, g).astype(jnp.int32), 1.0, 0.0)
            hits += hot
            weights[k:, at + j : at + j + LANES] = hot[:SLOTS].astype(jnp.bfloat16)
            g += 1
        at += sizes[s]
        upto = n if s == stages - 1 else at // TILE * TILE
        if upto - done >= 2 * TILE or upto == n:
            add = jnp.dot(weights[:, done:upto], rows[done:upto, :], preferred_element_type=jnp.float32)
            total = add if total is None else total + add
            done = upto
    for p in range(PEERS):
        sums[p, :part, :] = total[p * part : (p + 1) * part, :]
        sums[p, part:, :] = total[k + p * each : k + (p + 1) * each, :]
    mass = jnp.sum(heavy.T, axis=0, keepdims=True)
    hits = jnp.sum(hits.T, axis=0, keepdims=True)
    blank = jnp.zeros((1, LANES - part - each), jnp.float32)
    for p in range(PEERS):
        counts[p : p + 1, :] = jnp.concatenate(
            [mass[:, p * part : (p + 1) * part], hits[:, p * each : (p + 1) * each], blank], axis=1
        )


def sum_rows(groups, position, near, parts, expos, rows):
    k = expos[0].shape[0]
    width = rows[0].shape[1]
    sizes = tuple(r.shape[0] for r in rows)
    n = sum(sizes)
    in_vmem = pl.BlockSpec(memory_space=pltpu.VMEM)
    return pl.pallas_call(
        functools.partial(sum_kernel, groups, sizes),
        in_specs=[pl.BlockSpec(memory_space=pltpu.SMEM)] + [in_vmem] * (2 + 2 * len(sizes)),
        out_specs=(in_vmem, in_vmem),
        out_shape=(
            jax.ShapeDtypeStruct((PEERS, (k + SLOTS) // PEERS, width), jnp.float32),
            jax.ShapeDtypeStruct((PEERS, LANES), jnp.float32),
        ),
        scratch_shapes=[
            pltpu.VMEM((k + SLOTS, n), jnp.bfloat16),
            pltpu.VMEM((n, width), jnp.bfloat16),
            pltpu.VMEM((2, Z, LANES), jnp.float32),
            pltpu.VMEM((2, Z, LANES), jnp.float32),
        ],
        compiler_params=pltpu.CompilerParams(vmem_limit_bytes=20 * MIB),
        cost_estimate=pl.CostEstimate(
            flops=2 * (k + SLOTS) * width * n, bytes_accessed=2 * k * n + 2 * width * n, transcendentals=0
        ),
    )(position, near, parts, *expos, *rows)


def pack_kernel(kept, taken, kept_counts, taken_counts, out):
    count, width = kept.shape[1:]
    at = count * (width // LANES)
    counts = kept_counts[...] + taken_counts[...]
    high = counts.astype(jnp.bfloat16).astype(jnp.float32)
    low = counts - high
    for p in range(PEERS):
        rows = kept[p] + taken[p]
        size = jnp.max(jnp.abs(rows), axis=1, keepdims=True)
        exponent = jnp.clip(jnp.ceil(jnp.log2(jnp.maximum(size, 1e-30))), -100.0, 100.0)
        rows = rows * jnp.exp2(-exponent)
        for b in range(width // LANES):
            out[p, b * count : (b + 1) * count, :] = rows[:, b * LANES : (b + 1) * LANES]
        wide = jnp.concatenate(
            [jnp.broadcast_to(exponent, (count, LANES)), jnp.zeros((LANES - count, LANES), jnp.float32)]
        )
        out[p, at : at + 1, :] = wide.T[:1, :]
        out[p, at + 1 : at + 2, :] = high[p : p + 1, :]
        out[p, at + 2 : at + 3, :] = low[p : p + 1, :]


def packed_sums(kept, taken):
    _, count, width = kept[0].shape
    in_vmem = pl.BlockSpec(memory_space=pltpu.VMEM)
    return pl.pallas_call(
        pack_kernel,
        in_specs=[in_vmem] * 4,
        out_specs=in_vmem,
        out_shape=jax.ShapeDtypeStruct((PEERS, count * (width // LANES) + 3, LANES), jnp.float32),
        compiler_params=pltpu.CompilerParams(vmem_limit_bytes=8 * MIB),
    )(kept[0], taken[0], kept[1], taken[1])


def combine(first, second):
    top = jnp.maximum(first[0], second[0])
    total = first[1] * jnp.exp(first[0] - top) + second[1] * jnp.exp(second[0] - top)
    return jnp.stack([top, total, first[2] + second[2]])


def row_slots(section_codes, code_owner):
    codes = code_owner.shape[0]
    index = jnp.arange(codes, dtype=jnp.int32)
    same = (code_owner[:, None] == code_owner[None, :]) & (index[None, :] < index[:, None])
    code_slot = code_owner * SLOTS + jnp.sum(same.astype(jnp.int32), axis=1)
    hit = section_codes[:, None] == index[None, :]
    return jnp.sum(jnp.where(hit, code_slot[None, :], 0), axis=1)


def as_row(values):
    pad = [(0, 0)] * (values.ndim - 1) + [(0, LANES - values.shape[-1])]
    return jnp.pad(values, pad)[..., None, :].astype(jnp.float16)


def local(residuals, codebook, section_codes, code_owner):
    blk = lax.axis_index("blk")
    peer = lax.axis_index("dp")
    z, core = blk // C % Z, blk % C
    count, width = residuals.shape
    k = codebook.shape[0]
    half = count // 2

    def norm(book):
        return 0.5 * jnp.sum(jnp.square(book.astype(jnp.float32)), axis=1, keepdims=True)

    up, down = shifted(residuals, dz=1), shifted(residuals, dz=-1)
    other = shifted(codebook, dc=1)
    books, norms = (codebook, other), (norm(codebook), norm(other))

    groups, scored = [], []

    def stage(same, sides):
        sources, plan, at = [], [], 0
        for block, off in same:
            for piece in block:
                plan.append((len(sources), 0, piece.shape[0], at))
                sources.append(piece)
                at += piece.shape[0]
            groups.append((0, off % Z))
        if sides:
            first = len(sources)
            sources.extend(sides[:2])
            for i, off in enumerate(sides[2]):
                plan += [(first, i * half, half, at), (first + 1, i * half, half, at + half)]
                at += count
                groups.append((1, off % Z))
        scored.append(score_rows(books, norms, sources, tuple(plan)))

    def after(value, *earlier):
        return lax.optimization_barrier((value, earlier))[0]

    def across(blocks, *earlier):
        parts = after(
            (jnp.concatenate([b[:half] for b in blocks]), jnp.concatenate([b[half:] for b in blocks])), *earlier
        )
        return shifted(parts[0], dy=1), shifted(parts[1], dy=-1)

    stage([([residuals], 0), ([up], -1), ([down], 1)], None)
    sides = [across([residuals, up, down], scored[-1][3])]
    up, down = shifted(up, dz=1), shifted(down, dz=-1)
    up, down = after((up, down), scored[-1][3])
    stage([([up], -2), ([down], 2)], None)
    sides.append(across([up, down], scored[-1][3]))
    up, down = shifted(up, dz=1), shifted(down, dz=-1)
    up, down = after((up, down), scored[-1][3], *sides[0])
    stage([], (*sides[0], (0, -1, 1)))
    sides.append(across([up, down]))
    far = (shifted(up[:half], dz=1), shifted(down[half:], dz=-1))
    slots = row_slots(*after((section_codes, code_owner), scored[-1][3])).astype(jnp.float32)[None]
    far = after(far, *sides[1])
    last = (shifted(far[0], dy=1), shifted(far[1], dy=-1), (Z // 2,))
    stage([([up], -3), ([down], 3)], (*sides[1], (-2, 2)))
    stage([(list(far), Z // 2)], (*sides[2], (-3, 3)))
    stage([], last)

    position = jnp.stack([z, blk * SLOTS]).astype(jnp.int32)
    near = arrange(tuple(groups), position, slots, [s[3] for s in scored])
    stats = [near[:, 0], near[:, 1]]
    passed = shifted(stats[1], dy=-1), shifted(stats[0], dy=1)
    stats = jnp.stack([combine(stats[0], passed[0]), combine(stats[1], passed[1])], axis=1)
    same = [[(y * Z + at) * C + c for at in range(Z)] for y in range(2) for c in range(C)]
    stats = lax.all_to_all(
        jnp.broadcast_to(stats[None], (Z, *stats.shape)), "blk", 0, 0, axis_index_groups=same, tiled=True
    )

    rows = [s[2] for s in scored]
    flipped = position + jnp.stack([0, (1 - 2 * core) * SLOTS]).astype(jnp.int32)
    given = sum_rows(tuple(groups), flipped, near, stats, [s[1] for s in scored], rows)
    taken = [shifted(v, dc=1) for v in given]
    kept = sum_rows(tuple(groups), position, near, stats, [s[0] for s in scored], rows)
    part, slot_part = k // PEERS, SLOTS // PEERS
    got = lax.all_to_all(
        packed_sums(kept, taken).astype(jnp.float16), "dp", split_axis=0, concat_axis=0, tiled=True
    )
    both, cuts = part + slot_part, width // LANES
    full = cuts * both

    def unpacked(values):
        scales = jnp.exp2(values[:, full, :both].astype(jnp.float32))[:, None, :, None]
        return values[:, :full].reshape(PEERS, cuts, both, LANES), scales

    values, scales = unpacked(got)
    sums = jnp.sum(values.astype(jnp.float32) * scales, axis=0)
    counts = got[:, full + 1 : full + 3, :both].astype(jnp.float32)
    counts = jnp.sum(counts, axis=(0, 1))[None, :, None]
    prior = PRIOR * lax.dynamic_slice_in_dim(codebook, peer * part, part).astype(jnp.float32)
    prior = prior.reshape(part, cuts, LANES).transpose(1, 0, 2)
    result = jnp.concatenate(
        [
            (sums[:, :part] + prior) / (counts[:, :part] + PRIOR),
            sums[:, part:] / (counts[:, part:] + 1.0),
        ],
        axis=1,
    )
    size = jnp.max(jnp.abs(result), axis=(0, 2))
    exponent = jnp.clip(jnp.ceil(jnp.log2(jnp.maximum(size, 1e-30))), -100.0, 100.0)
    scaled = (result * jnp.exp2(-exponent)[None, :, None]).reshape(full, LANES)
    sent = jnp.concatenate([scaled.astype(jnp.float16), as_row(exponent)])
    got = lax.all_to_all(
        jnp.broadcast_to(sent[None], (PEERS, *sent.shape)), "dp", split_axis=0, concat_axis=0, tiled=True
    )
    values, scales = unpacked(got)

    def joined(lo, hi):
        rows = jnp.concatenate([values[:, i, lo:hi] for i in range(cuts)], axis=-1)
        return (rows.astype(jnp.float32) * scales[:, 0, lo:hi]).reshape(-1, width)

    return joined(0, part), joined(part, both)


def solution(mesh):
    in_specs = (P(("blk", "dp"), None), P("blk", None), P(("blk", "dp")), P())
    out_specs = (P("blk", None), P("blk", None))
    return jax.shard_map(local, mesh=mesh, in_specs=in_specs, out_specs=out_specs, check_vma=False)
```

time: 184 us -> 137 us (0.74); the launches traced: 181 us -> 137 us
  local copies, waits for them, and re-layouts: 40.3 us -> 2.7 us
  waiting for transfers between devices: 37.7 us -> 26.5 us
  blocking collectives: 24.9 us -> 33.6 us
  other arithmetic: 14.6 us -> 8.12 us
  starting transfers between devices: 41.7 us -> 45.6 us
    unnamed x108 -> x18, local copies, waits for them, and re-layouts: 33.2 us -> 1.14 us
    all_to_all x0 -> x1, blocking collectives: none -> 12.8 us  [local(): lax.all_to_all(jnp.broadcast_to(stats[None], (Z, *stats.shape)), 'blk', 0...]
    ppermute x3 -> x0, waiting for transfers between devices: 11.8 us -> none  [z_partner(): return lax.ppermute(value, AXES, pairs)]
    ppermute x22 -> x21, starting transfers between devices: 34.8 us -> 41.6 us  [shifted(): return lax.ppermute(value, AXES, pairs)]
    all_to_all x1, blocking collectives: 24.9 us -> 20.8 us  [local(): lax.all_to_all(jnp.broadcast_to(sent[None], (PEERS, *sent.shape)), 'dp',...]
    concatenate x7, other arithmetic: 3.42 us -> 0.26 us  [the longest x1 0.11 us: local(): jnp.concatenate([(sums[:, :part] + prior) / (counts[:, :part] + PRIOR), s...]
    all_to_all x1, waiting for transfers between devices: 16.7 us -> 19.5 us  [local(): lax.all_to_all(packed_sums(kept, taken).astype(jnp.float16), 'dp', split_...]
    mul x2 -> x4, other arithmetic: 0.24 us -> 2.62 us  [the longest x2 2.61 us: joined(): return (rows.astype(jnp.float32) * scales[:, 0, lo:hi]).reshape(-1, width)]
  transfers between devices with their start and end apart: 26 -> 22, of which waited for: 10 -> 8; matrix products, arithmetic and copies ran while one was open for 5% -> 2% of each run, Pallas kernels for 5% -> 9%
where the time goes in v2:
time: 137 us
  starting transfers between devices  45.6 us (33%)
  blocking collectives  33.6 us (25%)
  waiting for transfers between devices  26.5 us (19%)
  Pallas kernels  18.9 us (14%)
  other arithmetic  8.12 us (6%)
  local copies, waits for them, and re-layouts  2.7 us (2%)
    ppermute x21, starting transfers between devices, shifted(): return lax.ppermute(value, AXES, pairs)  41.6 us
    all_to_all x1, blocking collectives, local(): lax.all_to_all(jnp.broadcast_to(sent[None], (PEERS, *sent.shape)), 'dp',...  20.8 us
    all_to_all x1, waiting for transfers between devices, local(): lax.all_to_all(packed_sums(kept, taken).astype(jnp.float16), 'dp', split_...  19.5 us
    all_to_all x1, blocking collectives, local(): lax.all_to_all(jnp.broadcast_to(stats[None], (Z, *stats.shape)), 'blk', 0...  12.8 us
    pallas_call x6, Pallas kernels, score_rows(): pl.pallas_call(functools.partial(score_kernel, plan, len(sources)), in_sp...  9.89 us
    pallas_call x2, Pallas kernels, sum_rows(): pl.pallas_call(functools.partial(sum_kernel, groups, sizes), in_specs=[pl...  7.84 us
    ppermute x21, waiting for transfers between devices, shifted(): return lax.ppermute(value, AXES, pairs)  7 us
    all_to_all x1, starting transfers between devices, local(): lax.all_to_all(packed_sums(kept, taken).astype(jnp.float16), 'dp', split_...  4.02 us
  transfers between devices with their start and end apart: 22, of which 8 were waited for; matrix products, arithmetic and copies ran while one was open for 2% of the time, Pallas kernels for 9%

profile of v2, /device:TPU:1, one launch (start us, length us, event | category | flops | bytes accessed | tf_op | source)
XLA Modules:
  0.0 136.5 jit_solution(14097327082040520206)
XLA Ops:
  0.6 2.5 %collective-permute-start.1 = (bf16[128,768]{1,0:T(8,128)(2,1)}, bf16[128,768]{1,0:T(8,128)(2,1)S(1)}, u32[]{:S(2)}, u32[]{:S(2)}) collective-permute-start(bf16[128,768]{1,0:T(8,128)(2,1)} %refs_4_.1), channel_id=1, source_target_pairs={{0,16},{8,24},{16,32},{24,40},{32,48},{40,56},{48,64},{56,72},{64,... | collective-permute-start | bytes 589832 | tf_op jit(solution)/shard_map/ppermute | solution.py:37
  3.2 4.0 %collective-permute-start.2 = (bf16[128,768]{1,0:T(8,128)(2,1)}, bf16[128,768]{1,0:T(8,128)(2,1)S(1)}, u32[]{:S(2)}, u32[]{:S(2)}) collective-permute-start(bf16[128,768]{1,0:T(8,128)(2,1)} %refs_4_.1), channel_id=1, source_target_pairs={{0,112},{8,120},{16,0},{24,8},{32,16},{40,24},{48,32},{56,40},{64,... | collective-permute-start | bytes 589832 | tf_op jit(solution)/shard_map/ppermute | solution.py:37
  7.2 1.0 collective-permute-start
  8.2 1.6 %multiply_reduce_fusion.2 = f32[768]{0:T(1024)S(1)} fusion(bf16[768,768]{1,0:T(8,128)(2,1)} %refs_0_.11), kind=kLoop, calls=%fused_computation.6 | loop fusion | flops 1768704 | bytes 1182720 | tf_op jit(solution)/shard_map/reduce_sum | solution.py:277
  10.1 1.9 %collective-permute-done.1.refs_5_ = bf16[128,768]{1,0:T(8,128)(2,1)S(1)} collective-permute-done((bf16[128,768]{1,0:T(8,128)(2,1)}, bf16[128,768]{1,0:T(8,128)(2,1)S(1)}, u32[]{:S(2)}, u32[]{:S(2)}) %collective-permute-start.1) | collective-permute-done | bytes 196640 | tf_op jit(solution)/shard_map/ppermute | solution.py:37
  12.0 2.7 %collective-permute-start.6 = (bf16[128,768]{1,0:T(8,128)(2,1)S(1)}, bf16[128,768]{1,0:T(8,128)(2,1)S(1)}, u32[]{:S(2)}, u32[]{:S(2)}) collective-permute-start(bf16[128,768]{1,0:T(8,128)(2,1)S(1)} %collective-permute-done.2.refs_6_), channel_id=1, source_target_pairs={{0,112},{8,120},{16,0},{24,8},{32,16},{40,24},{48,32},{56,40},{64,... | collective-permute-start | bytes 589832 | tf_op jit(solution)/shard_map/ppermute | solution.py:37
  14.8 0.3 multiply_reduce_fusion.1
  15.2 0.7 copy-done
  16.0 1.9 %shard_map.59 = (bf16[768,384]{1,0:T(8,128)(2,1)S(1)}, bf16[768,384]{1,0:T(8,128)(2,1)S(1)}, bf16[384,768]{1,0:T(8,128)(2,1)S(1)}, f32[2,3,128]{2,1,0:T(4,128)S(1)}) custom-call(bf16[768,768]{1,0:T(8,128)(2,1)S(1)} %copy-done, bf16[768,768]{1,0:T(8,128)(2,1)S(1)} %collective-permute-done.refs_1_, f32[768,1]{1,0:T(8,128)S(1)} %mul.128.refs_2_, ...), custom_call_target="tpu_custom_call" | custom-call | flops 905969664 | bytes 3538944 | tf_op jit(solution)/shard_map/pallas_call | solution.py:81
  17.9 0.5 collective-permute-done.5.refs_4_
  18.3 2.7 %collective-permute-start.8 = (bf16[128,768]{1,0:T(8,128)(2,1)S(1)}, bf16[128,768]{1,0:T(8,128)(2,1)S(1)}, u32[]{:S(2)}, u32[]{:S(2)}) collective-permute-start(bf16[128,768]{1,0:T(8,128)(2,1)S(1)} %collective-permute-done.6.refs_5_), channel_id=1, source_target_pairs={{0,112},{8,120},{16,0},{24,8},{32,16},{40,24},{48,32},{56,40},{64,... | collective-permute-start | bytes 589832 | tf_op jit(solution)/shard_map/ppermute | solution.py:37
  21.0 1.3 collective-permute-start.3
  22.3 1.4 %collective-permute-start.4 = (bf16[192,768]{1,0:T(8,128)(2,1)S(1)}, bf16[192,768]{1,0:T(8,128)(2,1)S(1)}, u32[]{:S(2)}, u32[]{:S(2)}) collective-permute-start(bf16[192,768]{1,0:T(8,128)(2,1)S(1)} %get-tuple-element.46), channel_id=1, source_target_pairs={{0,129},{8,137},{16,145},{24,153},{32,161},{40,169},{48,177},{56,1... | collective-permute-start | bytes 884744 | tf_op jit(solution)/shard_map/ppermute | solution.py:37
  23.8 1.2 shard_map.61
  25.1 2.6 %collective-permute-start.10 = (bf16[128,768]{1,0:T(8,128)(2,1)S(1)}, bf16[128,768]{1,0:T(8,128)(2,1)S(1)}, u32[]{:S(2)}, u32[]{:S(2)}) collective-permute-start(bf16[128,768]{1,0:T(8,128)(2,1)S(1)} %pad_maximum_fusion.4), channel_id=1, source_target_pairs={{0,129},{8,137},{16,145},{24,153},{32,161},{40,169},{48,177},{56,1... | collective-permute-start | bytes 589832 | tf_op jit(solution)/shard_map/ppermute | solution.py:37
  27.9 0.3 collective-permute-done.4.refs_5_
  28.2 0.3 collective-permute-start.11
  28.5 2.7 %collective-permute-start.12 = (bf16[64,768]{1,0:T(8,128)(2,1)S(1)}, bf16[64,768]{1,0:T(8,128)(2,1)S(1)}, u32[]{:S(2)}, u32[]{:S(2)}) collective-permute-start(bf16[64,768]{1,0:T(8,128)(2,1)S(1)} %get-tuple-element.103), channel_id=1, source_target_pairs={{0,112},{8,120},{16,0},{24,8},{32,16},{40,24},{48,32},{56,40},{64,... | collective-permute-start | bytes 294920 | tf_op jit(solution)/shard_map/ppermute | solution.py:37
  31.3 1.4 %collective-permute-start.13 = (bf16[128,768]{1,0:T(8,128)(2,1)S(1)}, bf16[128,768]{1,0:T(8,128)(2,1)S(1)}, u32[]{:S(2)}, u32[]{:S(2)}) collective-permute-start(bf16[128,768]{1,0:T(8,128)(2,1)S(1)} %pad_maximum_fusion.5), channel_id=1, source_target_pairs={{0,128},{8,136},{16,144},{24,152},{32,160},{40,168},{48,176},{56,1... | collective-permute-start | bytes 589832 | tf_op jit(solution)/shard_map/ppermute | solution.py:37
  32.7 1.9 %shard_map.60 = (bf16[768,384]{1,0:T(8,128)(2,1)S(1)}, bf16[768,384]{1,0:T(8,128)(2,1)S(1)}, bf16[384,768]{1,0:T(8,128)(2,1)S(1)}, f32[2,3,128]{2,1,0:T(4,128)S(1)}) custom-call(bf16[768,768]{1,0:T(8,128)(2,1)S(1)} %copy-done, bf16[768,768]{1,0:T(8,128)(2,1)S(1)} %collective-permute-done.refs_1_, f32[768,1]{1,0:T(8,128)S(1)} %mul.128.refs_2_, ...), custom_call_target="tpu_custom_call" | custom-call | flops 905969664 | bytes 3538944 | tf_op jit(solution)/shard_map/pallas_call | solution.py:81
  34.6 0.5 convert_reduce_fusion
  35.1 0.2 select_reduce_fusion
  35.3 1.5 %collective-permute-start.14 = (bf16[128,768]{1,0:T(8,128)(2,1)S(1)}, bf16[128,768]{1,0:T(8,128)(2,1)S(1)}, u32[]{:S(2)}, u32[]{:S(2)}) collective-permute-start(bf16[128,768]{1,0:T(8,128)(2,1)S(1)} %pad_maximum_fusion.6), channel_id=1, source_target_pairs={{0,129},{8,137},{16,145},{24,153},{32,161},{40,169},{48,177},{56,1... | collective-permute-start | bytes 589832 | tf_op jit(solution)/shard_map/ppermute | solution.py:37
  36.8 0.2 collective-permute-start.15
  37.0 2.6 %collective-permute-start.16 = (bf16[64,768]{1,0:T(8,128)(2,1)S(1)}, bf16[64,768]{1,0:T(8,128)(2,1)S(1)}, u32[]{:S(2)}, u32[]{:S(2)}) collective-permute-start(bf16[64,768]{1,0:T(8,128)(2,1)S(1)} %collective-permute-done.12.refs_5_), channel_id=1, source_target_pairs={{0,129},{8,137},{16,145},{24,153},{32,161},{40,169},{48,177},{56,1... | collective-permute-start | bytes 294920 | tf_op jit(solution)/shard_map/ppermute | solution.py:37
  39.6 2.0 %shard_map.62 = (bf16[768,512]{1,0:T(8,128)(2,1)S(1)}, bf16[768,512]{1,0:T(8,128)(2,1)S(1)}, bf16[512,768]{1,0:T(8,128)(2,1)S(1)}, f32[2,4,128]{2,1,0:T(4,128)S(1)}) custom-call(bf16[768,768]{1,0:T(8,128)(2,1)S(1)} %copy-done, bf16[768,768]{1,0:T(8,128)(2,1)S(1)} %collective-permute-done.refs_1_, f32[768,1]{1,0:T(8,128)S(1)} %mul.128.refs_2_, ...), custom_call_target="tpu_custom_call" | custom-call | flops 1207959552 | bytes 3932160 | tf_op jit(solution)/shard_map/pallas_call | solution.py:81
  41.6 1.0 shard_map.64
  42.6 1.9 %shard_map.63 = (bf16[768,384]{1,0:T(8,128)(2,1)S(1)}, bf16[768,384]{1,0:T(8,128)(2,1)S(1)}, bf16[384,768]{1,0:T(8,128)(2,1)S(1)}, f32[2,3,128]{2,1,0:T(4,128)S(1)}) custom-call(bf16[768,768]{1,0:T(8,128)(2,1)S(1)} %copy-done, bf16[768,768]{1,0:T(8,128)(2,1)S(1)} %collective-permute-done.refs_1_, f32[768,1]{1,0:T(8,128)S(1)} %mul.128.refs_2_, ...), custom_call_target="tpu_custom_call" | custom-call | flops 905969664 | bytes 3538944 | tf_op jit(solution)/shard_map/pallas_call | solution.py:81
  44.5 0.6 shard_map.65.near
  45.1 2.7 %collective-permute-start.17 = (f32[3,8,128]{2,1,0:T(8,128)S(1)}, f32[3,8,128]{2,1,0:T(8,128)S(1)}, u32[]{:S(2)}, u32[]{:S(2)}) collective-permute-start(f32[3,8,128]{2,1,0:T(8,128)S(1)} %get-tuple-element.119), channel_id=1, source_target_pairs={{0,129},{8,137},{16,145},{24,153},{32,161},{40,169},{48,177},{56,1... | collective-permute-start | bytes 36872 | tf_op jit(solution)/shard_map/ppermute | solution.py:37
  47.8 0.8 collective-permute-done.17
  48.6 2.9 %collective-permute-done.18 = f32[3,8,128]{2,1,0:T(8,128)S(1)} collective-permute-done((f32[3,8,128]{2,1,0:T(8,128)S(1)}, f32[3,8,128]{2,1,0:T(8,128)S(1)}, u32[]{:S(2)}, u32[]{:S(2)}) %collective-permute-start.18) | collective-permute-done | bytes 12320 | tf_op jit(solution)/shard_map/ppermute | solution.py:37
  51.6 12.8 %all_to_all.15.parts = f32[8,3,2,8,128]{4,3,2,1,0:T(8,128)S(1)} all-to-all(f32[8,3,2,8,128]{4,3,2,1,0:T(8,128)S(1)} %broadcast_in_dim.20), channel_id=1, replica_groups={{0,16,32,48,64,80,96,112},{8,24,40,56,72,88,104,120},{128,144,160,176,1..., dimensions={0} | all-to-all | bytes 393216 | tf_op jit(solution)/shard_map/all_to_all | solution.py:335
  64.4 3.9 %shard_map.67 = (f32[8,104,768]{2,1,0:T(8,128)S(1)}, f32[8,128]{1,0:T(8,128)S(1)}) custom-call(s32[2]{0:T(128)S(1)} %get-tuple-element.86.position, f32[3,2,8,128]{3,2,1,0:T(8,128)S(1)} %shard_map.65.near, f32[8,3,2,8,128]{4,3,2,1,0:T(8,128)S(1)} %all_to_all.15.parts, bf16[768,384]{1,0:T(8,128)(2,1)S(1)} %get-tuple-element.77.refs_0_, ...), custom_call_target="tpu_custom_call" | custom-call | flops 2617245696 | bytes 6291456 | tf_op jit(solution)/shard_map/pallas_call | solution.py:194
  68.3 11.8 %collective-permute-start.19 = (f32[8,104,768]{2,1,0:T(8,128)S(1)}, f32[8,104,768]{2,1,0:T(8,128)S(1)}, u32[]{:S(2)}, u32[]{:S(2)}) collective-permute-start(f32[8,104,768]{2,1,0:T(8,128)S(1)} %get-tuple-element.83), channel_id=1, source_target_pairs={{0,8},{8,0},{16,24},{24,16},{32,40},{40,32},{48,56},{56,48},{64,72... | collective-permute-start | bytes 7667720 | tf_op jit(solution)/shard_map/ppermute | solution.py:37
  80.3 3.9 %shard_map.66 = (f32[8,104,768]{2,1,0:T(8,128)S(1)}, f32[8,128]{1,0:T(8,128)S(1)}) custom-call(s32[2]{0:T(128)S(1)} %get-tuple-element.87.position, f32[3,2,8,128]{3,2,1,0:T(8,128)S(1)} %shard_map.65.near, f32[8,3,2,8,128]{4,3,2,1,0:T(8,128)S(1)} %all_to_all.15.parts, bf16[768,384]{1,0:T(8,128)(2,1)S(1)} %get-tuple-element.64.refs_0_, ...), custom_call_target="tpu_custom_call" | custom-call | flops 2617245696 | bytes 6291456 | tf_op jit(solution)/shard_map/pallas_call | solution.py:194
  84.2 0.4 collective-permute-done.20.taken_counts
  84.6 0.6 shard_map.68
  85.2 1.2 convert_element_type.76
  86.4 4.0 %all-to-all-start.1 = ((f16[8,627,128]{2,1,0:T(8,128)(2,1)}), f16[8,627,128]{2,1,0:T(8,128)(2,1)S(1)}, u32[]{:S(2)}, u32[]{:S(2)}) async-start(f16[8,627,128]{2,1,0:T(8,128)(2,1)} %convert_element_type.76), calls=%async_computation.1 | async-start | bytes 2588672 | tf_op jit(solution)/shard_map/all_to_all | solution.py:345
  90.4 19.5 %all-to-all-done.1 = f16[8,627,128]{2,1,0:T(8,128)(2,1)S(1)} async-done(((f16[8,627,128]{2,1,0:T(8,128)(2,1)}), f16[8,627,128]{2,1,0:T(8,128)(2,1)S(1)}, u32[]{:S(2)}, u32[]{:S(2)}) %all-to-all-start.1) | async-done | bytes 1284128 | tf_op jit(solution)/shard_map/all_to_all | solution.py:345
  110.1 0.8 multiply_reduce_fusion
  111.6 0.2 broadcast_in_dim.22
  111.8 20.8 %all_to_all.16 = f16[8,625,128]{2,1,0:T(8,128)(2,1)S(1)} all-to-all(f16[8,625,128]{2,1,0:T(8,128)(2,1)S(1)} %broadcast_in_dim.22), channel_id=1, replica_groups=mesh['blk'=32,'dp'=8] {'dp'}, dimensions={0} | all-to-all | bytes 2560000 | tf_op jit(solution)/shard_map/all_to_all | solution.py:372
  132.6 0.2 slice.245
  132.9 0.2 fusion.17
  133.5 0.8 convert_multiply_fusion.1
  134.7 1.9 %convert_multiply_fusion = f32[768,768]{1,0:T(8,128)} fusion(f16[768,768]{1,0:T(8,128)(2,1)S(1)} %constant_dynamic-update-slice_fusion, f32[768]{0:T(1024)S(1)} %mul.122), kind=kLoop, calls=%fused_computation.4 | loop fusion | flops 1179648 | bytes 3542016 | tf_op jit(solution)/shard_map/mul | solution.py:379
  (83 shorter events, 2.5 us)
Async XLA Ops:
  0.6 9.4 %copy-start.1 = (bf16[128,768]{1,0:T(8,128)(2,1)S(1)}, bf16[128,768]{1,0:T(8,128)(2,1)}, u32[]{:S(2)}) copy-start(bf16[128,768]{1,0:T(8,128)(2,1)} %refs_4_.1) | copy-start | bytes 589828
  0.6 11.3 %collective-permute-start.1 = (bf16[128,768]{1,0:T(8,128)(2,1)}, bf16[128,768]{1,0:T(8,128)(2,1)S(1)}, u32[]{:S(2)}, u32[]{:S(2)}) collective-permute-start(bf16[128,768]{1,0:T(8,128)(2,1)} %refs_4_.1), channel_id=1, source_target_pairs={{0,16},{8,24},{16,32},{24,40},{32,48},{40,56},{48,64},{56,72},{64,... | collective-permute-start | bytes 589832 | tf_op jit(solution)/shard_map/ppermute | solution.py:37
  3.2 8.8 %collective-permute-start.2 = (bf16[128,768]{1,0:T(8,128)(2,1)}, bf16[128,768]{1,0:T(8,128)(2,1)S(1)}, u32[]{:S(2)}, u32[]{:S(2)}) collective-permute-start(bf16[128,768]{1,0:T(8,128)(2,1)} %refs_4_.1), channel_id=1, source_target_pairs={{0,112},{8,120},{16,0},{24,8},{32,16},{40,24},{48,32},{56,40},{64,... | collective-permute-start | bytes 589832 | tf_op jit(solution)/shard_map/ppermute | solution.py:37
  7.2 7.5 %collective-permute-start = (bf16[768,768]{1,0:T(8,128)(2,1)}, bf16[768,768]{1,0:T(8,128)(2,1)S(1)}, u32[]{:S(2)}, u32[]{:S(2)}) collective-permute-start(bf16[768,768]{1,0:T(8,128)(2,1)} %refs_0_.11), channel_id=1, source_target_pairs={{0,8},{8,0},{16,24},{24,16},{32,40},{40,32},{48,56},{56,48},{64,72... | collective-permute-start | bytes 3538952 | tf_op jit(solution)/shard_map/ppermute | solution.py:37
  12.0 6.4 %collective-permute-start.5 = (bf16[128,768]{1,0:T(8,128)(2,1)S(1)}, bf16[128,768]{1,0:T(8,128)(2,1)S(1)}, u32[]{:S(2)}, u32[]{:S(2)}) collective-permute-start(bf16[128,768]{1,0:T(8,128)(2,1)S(1)} %collective-permute-done.1.refs_5_), channel_id=1, source_target_pairs={{0,16},{8,24},{16,32},{24,40},{32,48},{40,56},{48,64},{56,72},{64,... | collective-permute-start | bytes 589832 | tf_op jit(solution)/shard_map/ppermute | solution.py:37
  12.0 6.4 %collective-permute-start.6 = (bf16[128,768]{1,0:T(8,128)(2,1)S(1)}, bf16[128,768]{1,0:T(8,128)(2,1)S(1)}, u32[]{:S(2)}, u32[]{:S(2)}) collective-permute-start(bf16[128,768]{1,0:T(8,128)(2,1)S(1)} %collective-permute-done.2.refs_6_), channel_id=1, source_target_pairs={{0,112},{8,120},{16,0},{24,8},{32,16},{40,24},{48,32},{56,40},{64,... | collective-permute-start | bytes 589832 | tf_op jit(solution)/shard_map/ppermute | solution.py:37
  14.7 1.3 copy-start
  18.3 6.8 %collective-permute-start.7 = (bf16[128,768]{1,0:T(8,128)(2,1)S(1)}, bf16[128,768]{1,0:T(8,128)(2,1)S(1)}, u32[]{:S(2)}, u32[]{:S(2)}) collective-permute-start(bf16[128,768]{1,0:T(8,128)(2,1)S(1)} %collective-permute-done.5.refs_4_), channel_id=1, source_target_pairs={{0,16},{8,24},{16,32},{24,40},{32,48},{40,56},{48,64},{56,72},{64,... | collective-permute-start | bytes 589832 | tf_op jit(solution)/shard_map/ppermute | solution.py:37
  18.3 9.4 %collective-permute-start.8 = (bf16[128,768]{1,0:T(8,128)(2,1)S(1)}, bf16[128,768]{1,0:T(8,128)(2,1)S(1)}, u32[]{:S(2)}, u32[]{:S(2)}) collective-permute-start(bf16[128,768]{1,0:T(8,128)(2,1)S(1)} %collective-permute-done.6.refs_5_), channel_id=1, source_target_pairs={{0,112},{8,120},{16,0},{24,8},{32,16},{40,24},{48,32},{56,40},{64,... | collective-permute-start | bytes 589832 | tf_op jit(solution)/shard_map/ppermute | solution.py:37
  21.0 6.8 %collective-permute-start.3 = (bf16[192,768]{1,0:T(8,128)(2,1)S(1)}, bf16[192,768]{1,0:T(8,128)(2,1)S(1)}, u32[]{:S(2)}, u32[]{:S(2)}) collective-permute-start(bf16[192,768]{1,0:T(8,128)(2,1)S(1)} %get-tuple-element.45), channel_id=1, source_target_pairs={{0,128},{8,136},{16,144},{24,152},{32,160},{40,168},{48,176},{56,1... | collective-permute-start | bytes 884744 | tf_op jit(solution)/shard_map/ppermute | solution.py:37
  22.3 5.9 %collective-permute-start.4 = (bf16[192,768]{1,0:T(8,128)(2,1)S(1)}, bf16[192,768]{1,0:T(8,128)(2,1)S(1)}, u32[]{:S(2)}, u32[]{:S(2)}) collective-permute-start(bf16[192,768]{1,0:T(8,128)(2,1)S(1)} %get-tuple-element.46), channel_id=1, source_target_pairs={{0,129},{8,137},{16,145},{24,153},{32,161},{40,169},{48,177},{56,1... | collective-permute-start | bytes 884744 | tf_op jit(solution)/shard_map/ppermute | solution.py:37
  25.0 10.3 %collective-permute-start.9 = (bf16[128,768]{1,0:T(8,128)(2,1)S(1)}, bf16[128,768]{1,0:T(8,128)(2,1)S(1)}, u32[]{:S(2)}, u32[]{:S(2)}) collective-permute-start(bf16[128,768]{1,0:T(8,128)(2,1)S(1)} %pad_maximum_fusion.3), channel_id=1, source_target_pairs={{0,128},{8,136},{16,144},{24,152},{32,160},{40,168},{48,176},{56,1... | collective-permute-start | bytes 589832 | tf_op jit(solution)/shard_map/ppermute | solution.py:37
  25.1 11.7 %collective-permute-start.10 = (bf16[128,768]{1,0:T(8,128)(2,1)S(1)}, bf16[128,768]{1,0:T(8,128)(2,1)S(1)}, u32[]{:S(2)}, u32[]{:S(2)}) collective-permute-start(bf16[128,768]{1,0:T(8,128)(2,1)S(1)} %pad_maximum_fusion.4), channel_id=1, source_target_pairs={{0,129},{8,137},{16,145},{24,153},{32,161},{40,169},{48,177},{56,1... | collective-permute-start | bytes 589832 | tf_op jit(solution)/shard_map/ppermute | solution.py:37
  28.2 8.6 %collective-permute-start.11 = (bf16[64,768]{1,0:T(8,128)(2,1)S(1)}, bf16[64,768]{1,0:T(8,128)(2,1)S(1)}, u32[]{:S(2)}, u32[]{:S(2)}) collective-permute-start(bf16[64,768]{1,0:T(8,128)(2,1)S(1)} %get-tuple-element.101), channel_id=1, source_target_pairs={{0,16},{8,24},{16,32},{24,40},{32,48},{40,56},{48,64},{56,72},{64,... | collective-permute-start | bytes 294920 | tf_op jit(solution)/shard_map/ppermute | solution.py:37
  28.5 8.3 %collective-permute-start.12 = (bf16[64,768]{1,0:T(8,128)(2,1)S(1)}, bf16[64,768]{1,0:T(8,128)(2,1)S(1)}, u32[]{:S(2)}, u32[]{:S(2)}) collective-permute-start(bf16[64,768]{1,0:T(8,128)(2,1)S(1)} %get-tuple-element.103), channel_id=1, source_target_pairs={{0,112},{8,120},{16,0},{24,8},{32,16},{40,24},{48,32},{56,40},{64,... | collective-permute-start | bytes 294920 | tf_op jit(solution)/shard_map/ppermute | solution.py:37
  31.3 3.3 %copy-start.2 = (s32[1024]{0:T(1024)S(1)}, s32[1024]{0:T(1024)}, u32[]{:S(2)}) copy-start(s32[1024]{0:T(1024)} %param.7) | copy-start | bytes 12292
  31.3 3.8 %copy-start.3 = (s32[128]{0:T(128)S(1)}, s32[128]{0:T(128)}, u32[]{:S(2)}) copy-start(s32[128]{0:T(128)} %param.6) | copy-start | bytes 1540
  31.3 11.3 %collective-permute-start.13 = (bf16[128,768]{1,0:T(8,128)(2,1)S(1)}, bf16[128,768]{1,0:T(8,128)(2,1)S(1)}, u32[]{:S(2)}, u32[]{:S(2)}) collective-permute-start(bf16[128,768]{1,0:T(8,128)(2,1)S(1)} %pad_maximum_fusion.5), channel_id=1, source_target_pairs={{0,128},{8,136},{16,144},{24,152},{32,160},{40,168},{48,176},{56,1... | collective-permute-start | bytes 589832 | tf_op jit(solution)/shard_map/ppermute | solution.py:37
  35.3 7.3 %collective-permute-start.14 = (bf16[128,768]{1,0:T(8,128)(2,1)S(1)}, bf16[128,768]{1,0:T(8,128)(2,1)S(1)}, u32[]{:S(2)}, u32[]{:S(2)}) collective-permute-start(bf16[128,768]{1,0:T(8,128)(2,1)S(1)} %pad_maximum_fusion.6), channel_id=1, source_target_pairs={{0,129},{8,137},{16,145},{24,153},{32,161},{40,169},{48,177},{56,1... | collective-permute-start | bytes 589832 | tf_op jit(solution)/shard_map/ppermute | solution.py:37
  36.8 4.8 %collective-permute-start.15 = (bf16[64,768]{1,0:T(8,128)(2,1)S(1)}, bf16[64,768]{1,0:T(8,128)(2,1)S(1)}, u32[]{:S(2)}, u32[]{:S(2)}) collective-permute-start(bf16[64,768]{1,0:T(8,128)(2,1)S(1)} %collective-permute-done.11.refs_4_), channel_id=1, source_target_pairs={{0,128},{8,136},{16,144},{24,152},{32,160},{40,168},{48,176},{56,1... | collective-permute-start | bytes 294920 | tf_op jit(solution)/shard_map/ppermute | solution.py:37
  37.0 4.6 %collective-permute-start.16 = (bf16[64,768]{1,0:T(8,128)(2,1)S(1)}, bf16[64,768]{1,0:T(8,128)(2,1)S(1)}, u32[]{:S(2)}, u32[]{:S(2)}) collective-permute-start(bf16[64,768]{1,0:T(8,128)(2,1)S(1)} %collective-permute-done.12.refs_5_), channel_id=1, source_target_pairs={{0,129},{8,137},{16,145},{24,153},{32,161},{40,169},{48,177},{56,1... | collective-permute-start | bytes 294920 | tf_op jit(solution)/shard_map/ppermute | solution.py:37
  45.1 3.5 %collective-permute-start.17 = (f32[3,8,128]{2,1,0:T(8,128)S(1)}, f32[3,8,128]{2,1,0:T(8,128)S(1)}, u32[]{:S(2)}, u32[]{:S(2)}) collective-permute-start(f32[3,8,128]{2,1,0:T(8,128)S(1)} %get-tuple-element.119), channel_id=1, source_target_pairs={{0,129},{8,137},{16,145},{24,153},{32,161},{40,169},{48,177},{56,1... | collective-permute-start | bytes 36872 | tf_op jit(solution)/shard_map/ppermute | solution.py:37
  47.8 3.8 %collective-permute-start.18 = (f32[3,8,128]{2,1,0:T(8,128)S(1)}, f32[3,8,128]{2,1,0:T(8,128)S(1)}, u32[]{:S(2)}, u32[]{:S(2)}) collective-permute-start(f32[3,8,128]{2,1,0:T(8,128)S(1)} %get-tuple-element.120), channel_id=1, source_target_pairs={{0,128},{8,136},{16,144},{24,152},{32,160},{40,168},{48,176},{56,1... | collective-permute-start | bytes 36872 | tf_op jit(solution)/shard_map/ppermute | solution.py:37
  68.3 16.3 %collective-permute-start.19 = (f32[8,104,768]{2,1,0:T(8,128)S(1)}, f32[8,104,768]{2,1,0:T(8,128)S(1)}, u32[]{:S(2)}, u32[]{:S(2)}) collective-permute-start(f32[8,104,768]{2,1,0:T(8,128)S(1)} %get-tuple-element.83), channel_id=1, source_target_pairs={{0,8},{8,0},{16,24},{24,16},{32,40},{40,32},{48,56},{56,48},{64,72... | collective-permute-start | bytes 7667720 | tf_op jit(solution)/shard_map/ppermute | solution.py:37
  80.2 4.4 %collective-permute-start.20 = (f32[8,128]{1,0:T(8,128)S(1)}, f32[8,128]{1,0:T(8,128)S(1)}, u32[]{:S(2)}, u32[]{:S(2)}) collective-permute-start(f32[8,128]{1,0:T(8,128)S(1)} %get-tuple-element.85), channel_id=1, source_target_pairs={{0,8},{8,0},{16,24},{24,16},{32,40},{40,32},{48,56},{56,48},{64,72... | collective-permute-start | bytes 12296 | tf_op jit(solution)/shard_map/ppermute | solution.py:37
  86.4 23.5 %all-to-all-start.1 = ((f16[8,627,128]{2,1,0:T(8,128)(2,1)}), f16[8,627,128]{2,1,0:T(8,128)(2,1)S(1)}, u32[]{:S(2)}, u32[]{:S(2)}) async-start(f16[8,627,128]{2,1,0:T(8,128)(2,1)} %convert_element_type.76), calls=%async_computation.1 | async-start | bytes 2588672 | tf_op jit(solution)/shard_map/all_to_all | solution.py:345

commit v3 on v2

--- a/solution.py
+++ b/solution.py
@@ -169,7 +169,7 @@
             g += 1
         at += sizes[s]
         upto = n if s == stages - 1 else at // TILE * TILE
-        if upto - done >= 2 * TILE or upto == n:
+        if upto - done >= 4 * TILE or upto == n:
             add = jnp.dot(weights[:, done:upto], rows[done:upto, :], preferred_element_type=jnp.float32)
             total = add if total is None else total + add
             done = upto
@@ -282,7 +282,7 @@
 
     groups, scored = [], []
 
-    def stage(same, sides):
+    def stage(same, *sides):
         sources, plan, at = [], [], 0
         for block, off in same:
             for piece in block:
@@ -290,10 +290,10 @@
                 sources.append(piece)
                 at += piece.shape[0]
             groups.append((0, off % Z))
-        if sides:
+        for lower, upper, offs in sides:
             first = len(sources)
-            sources.extend(sides[:2])
-            for i, off in enumerate(sides[2]):
+            sources.extend((lower, upper))
+            for i, off in enumerate(offs):
                 plan += [(first, i * half, half, at), (first + 1, i * half, half, at + half)]
                 at += count
                 groups.append((1, off % Z))
@@ -308,23 +308,22 @@
         )
         return shifted(parts[0], dy=1), shifted(parts[1], dy=-1)
 
-    stage([([residuals], 0), ([up], -1), ([down], 1)], None)
-    sides = [across([residuals, up, down], scored[-1][3])]
-    up, down = shifted(up, dz=1), shifted(down, dz=-1)
+    stage([([up], -1), ([down], 1)])
+    near_side = across([residuals, up, down], scored[-1][3])
+    up_two, down_two = after((shifted(up, dz=1), shifted(down, dz=-1)), scored[-1][3])
+    stage([([up_two], -2), ([down_two], 2)])
+    up, down = after((shifted(up_two, dz=1), shifted(down_two, dz=-1)), scored[-1][3])
+    far = (shifted(up[:half], dz=1), shifted(down[half:], dz=-1))
+    side = across([up_two, down_two, up, down])
+    stage([([residuals], 0)], (*near_side, (0, -1, 1)))
+    slots = row_slots(*after((section_codes, code_owner), scored[-1][3])).astype(jnp.float32)[None]
+    far = after(far, scored[-1][3])
+    far_side = (shifted(far[0], dy=1), shifted(far[1], dy=-1))
     up, down = after((up, down), scored[-1][3])
-    stage([([up], -2), ([down], 2)], None)
-    sides.append(across([up, down], scored[-1][3]))
-    up, down = shifted(up, dz=1), shifted(down, dz=-1)
-    up, down = after((up, down), scored[-1][3], *sides[0])
-    stage([], (*sides[0], (0, -1, 1)))
-    sides.append(across([up, down]))
-    far = (shifted(up[:half], dz=1), shifted(down[half:], dz=-1))
-    slots = row_slots(*after((section_codes, code_owner), scored[-1][3])).astype(jnp.float32)[None]
-    far = after(far, *sides[1])
-    last = (shifted(far[0], dy=1), shifted(far[1], dy=-1), (Z // 2,))
-    stage([([up], -3), ([down], 3)], (*sides[1], (-2, 2)))
-    stage([(list(far), Z // 2)], (*sides[2], (-3, 3)))
-    stage([], last)
+    stage([([up], -3), ([down], 3)])
+    stage([], (*side, (-2, 2, -3, 3)))
+    far_side = after(far_side, scored[-1][3])
+    stage([(list(far), Z // 2)], (*far_side, (Z // 2,)))
 
     position = jnp.stack([z, blk * SLOTS]).astype(jnp.int32)
     near = arrange(tuple(groups), position, slots, [s[3] for s in scored])

time: 137 us -> 129 us (0.942)
  starting transfers between devices: 45.6 us -> 38.8 us
  Pallas kernels: 18.9 us -> 17.2 us
    ppermute x21 -> x19, starting transfers between devices: 41.6 us -> 34.8 us  [shifted(): return lax.ppermute(value, AXES, pairs)]
    ppermute x21 -> x19, waiting for transfers between devices: 7 us -> 7.56 us  [shifted(): return lax.ppermute(value, AXES, pairs)]
  transfers between devices with their start and end apart: 22 -> 20, of which waited for: 8 -> 6; matrix products, arithmetic and copies ran while one was open for 2% -> 2% of each run, Pallas kernels for 9% -> 9%
where the time goes in v3:
time: 129 us
  starting transfers between devices  38.8 us (30%)
  blocking collectives  33.9 us (26%)
  waiting for transfers between devices  27 us (21%)
  Pallas kernels  17.2 us (13%)
  other arithmetic  8.12 us (6%)
  local copies, waits for them, and re-layouts  2.71 us (2%)
    ppermute x19, starting transfers between devices, shifted(): return lax.ppermute(value, AXES, pairs)  34.8 us
    all_to_all x1, blocking collectives, local(): lax.all_to_all(jnp.broadcast_to(sent[None], (PEERS, *sent.shape)), 'dp',...  20.8 us
    all_to_all x1, waiting for transfers between devices, local(): lax.all_to_all(packed_sums(kept, taken).astype(jnp.float16), 'dp', split_...  19.5 us
    all_to_all x1, blocking collectives, local(): lax.all_to_all(jnp.broadcast_to(stats[None], (Z, *stats.shape)), 'blk', 0...  13 us
    pallas_call x6, Pallas kernels, score_rows(): pl.pallas_call(functools.partial(score_kernel, plan, len(sources)), in_sp...  8.7 us
    ppermute x19, waiting for transfers between devices, shifted(): return lax.ppermute(value, AXES, pairs)  7.56 us
    pallas_call x2, Pallas kernels, sum_rows(): pl.pallas_call(functools.partial(sum_kernel, groups, sizes), in_specs=[pl...  7.37 us
    all_to_all x1, starting transfers between devices, local(): lax.all_to_all(packed_sums(kept, taken).astype(jnp.float16), 'dp', split_...  4.04 us
  transfers between devices with their start and end apart: 20, of which 6 were waited for; matrix products, arithmetic and copies ran while one was open for 2% of the time, Pallas kernels for 9%

profile of v3, /device:TPU:1, one launch (start us, length us, event | category | flops | bytes accessed | tf_op | source)
XLA Modules:
  0.0 128.9 jit_solution(13312840167701650324)
XLA Ops:
  0.6 2.5 %collective-permute-start.1 = (bf16[128,768]{1,0:T(8,128)(2,1)}, bf16[128,768]{1,0:T(8,128)(2,1)S(1)}, u32[]{:S(2)}, u32[]{:S(2)}) collective-permute-start(bf16[128,768]{1,0:T(8,128)(2,1)} %refs_4_.1), channel_id=1, source_target_pairs={{0,16},{8,24},{16,32},{24,40},{32,48},{40,56},{48,64},{56,72},{64,... | collective-permute-start | bytes 589832 | tf_op jit(solution)/shard_map/ppermute | solution.py:37
  3.2 4.0 %collective-permute-start.2 = (bf16[128,768]{1,0:T(8,128)(2,1)}, bf16[128,768]{1,0:T(8,128)(2,1)S(1)}, u32[]{:S(2)}, u32[]{:S(2)}) collective-permute-start(bf16[128,768]{1,0:T(8,128)(2,1)} %refs_4_.1), channel_id=1, source_target_pairs={{0,112},{8,120},{16,0},{24,8},{32,16},{40,24},{48,32},{56,40},{64,... | collective-permute-start | bytes 589832 | tf_op jit(solution)/shard_map/ppermute | solution.py:37
  7.2 1.0 collective-permute-start
  8.2 1.6 %multiply_reduce_fusion.2 = f32[768]{0:T(1024)S(1)} fusion(bf16[768,768]{1,0:T(8,128)(2,1)} %refs_0_.11), kind=kLoop, calls=%fused_computation.6 | loop fusion | flops 1768704 | bytes 1182720 | tf_op jit(solution)/shard_map/reduce_sum | solution.py:277
  9.8 0.2 mul.128.refs_2_
  10.1 1.9 %collective-permute-done.1.refs_4_ = bf16[128,768]{1,0:T(8,128)(2,1)S(1)} collective-permute-done((bf16[128,768]{1,0:T(8,128)(2,1)}, bf16[128,768]{1,0:T(8,128)(2,1)S(1)}, u32[]{:S(2)}, u32[]{:S(2)}) %collective-permute-start.1) | collective-permute-done | bytes 196640 | tf_op jit(solution)/shard_map/ppermute | solution.py:37
  12.0 2.7 %collective-permute-start.6 = (bf16[128,768]{1,0:T(8,128)(2,1)S(1)}, bf16[128,768]{1,0:T(8,128)(2,1)S(1)}, u32[]{:S(2)}, u32[]{:S(2)}) collective-permute-start(bf16[128,768]{1,0:T(8,128)(2,1)S(1)} %collective-permute-done.2.refs_5_), channel_id=1, source_target_pairs={{0,112},{8,120},{16,0},{24,8},{32,16},{40,24},{48,32},{56,40},{64,... | collective-permute-start | bytes 589832 | tf_op jit(solution)/shard_map/ppermute | solution.py:37
  14.8 0.3 multiply_reduce_fusion.1
  15.1 0.2 mul.129.refs_3_
  15.2 0.7 copy-done
  16.0 1.2 shard_map.59
  17.1 1.2 collective-permute-done.5.refs_4_
  18.3 2.7 %collective-permute-start.8 = (bf16[128,768]{1,0:T(8,128)(2,1)S(1)}, bf16[128,768]{1,0:T(8,128)(2,1)S(1)}, u32[]{:S(2)}, u32[]{:S(2)}) collective-permute-start(bf16[128,768]{1,0:T(8,128)(2,1)S(1)} %collective-permute-done.6.refs_5_), channel_id=1, source_target_pairs={{0,112},{8,120},{16,0},{24,8},{32,16},{40,24},{48,32},{56,40},{64,... | collective-permute-start | bytes 589832 | tf_op jit(solution)/shard_map/ppermute | solution.py:37
  21.0 1.3 %collective-permute-start.3 = (bf16[192,768]{1,0:T(8,128)(2,1)S(1)}, bf16[192,768]{1,0:T(8,128)(2,1)S(1)}, u32[]{:S(2)}, u32[]{:S(2)}) collective-permute-start(bf16[192,768]{1,0:T(8,128)(2,1)S(1)} %get-tuple-element.47), channel_id=1, source_target_pairs={{0,128},{8,136},{16,144},{24,152},{32,160},{40,168},{48,176},{56,1... | collective-permute-start | bytes 884744 | tf_op jit(solution)/shard_map/ppermute | solution.py:37
  22.3 1.4 %collective-permute-start.4 = (bf16[192,768]{1,0:T(8,128)(2,1)S(1)}, bf16[192,768]{1,0:T(8,128)(2,1)S(1)}, u32[]{:S(2)}, u32[]{:S(2)}) collective-permute-start(bf16[192,768]{1,0:T(8,128)(2,1)S(1)} %get-tuple-element.48), channel_id=1, source_target_pairs={{0,129},{8,137},{16,145},{24,153},{32,161},{40,169},{48,177},{56,1... | collective-permute-start | bytes 884744 | tf_op jit(solution)/shard_map/ppermute | solution.py:37
  23.8 1.2 shard_map.61
  25.0 0.6 collective-permute-start.11
  25.6 2.2 %collective-permute-start.12 = (bf16[64,768]{1,0:T(8,128)(2,1)S(1)}, bf16[64,768]{1,0:T(8,128)(2,1)S(1)}, u32[]{:S(2)}, u32[]{:S(2)}) collective-permute-start(bf16[64,768]{1,0:T(8,128)(2,1)S(1)} %get-tuple-element.110), channel_id=1, source_target_pairs={{0,112},{8,120},{16,0},{24,8},{32,16},{40,24},{48,32},{56,40},{64,... | collective-permute-start | bytes 294920 | tf_op jit(solution)/shard_map/ppermute | solution.py:37
  27.9 0.5 collective-permute-start.9
  28.4 2.3 %collective-permute-start.10 = (bf16[256,768]{1,0:T(8,128)(2,1)S(1)}, bf16[256,768]{1,0:T(8,128)(2,1)S(1)}, u32[]{:S(2)}, u32[]{:S(2)}) collective-permute-start(bf16[256,768]{1,0:T(8,128)(2,1)S(1)} %pad_maximum_fusion.1), channel_id=1, source_target_pairs={{0,129},{8,137},{16,145},{24,153},{32,161},{40,169},{48,177},{56,1... | collective-permute-start | bytes 1179656 | tf_op jit(solution)/shard_map/ppermute | solution.py:37
  30.7 2.0 %shard_map.60 = (bf16[768,512]{1,0:T(8,128)(2,1)S(1)}, bf16[768,512]{1,0:T(8,128)(2,1)S(1)}, bf16[512,768]{1,0:T(8,128)(2,1)S(1)}, f32[2,4,128]{2,1,0:T(4,128)S(1)}) custom-call(bf16[768,768]{1,0:T(8,128)(2,1)S(1)} %copy-done, bf16[768,768]{1,0:T(8,128)(2,1)S(1)} %collective-permute-done.refs_1_, f32[768,1]{1,0:T(8,128)S(1)} %mul.128.refs_2_, ...), custom_call_target="tpu_custom_call" | custom-call | flops 1207959552 | bytes 3932160 | tf_op jit(solution)/shard_map/pallas_call | solution.py:81
  32.7 0.5 convert_reduce_fusion
  33.4 2.7 %collective-permute-start.14 = (bf16[64,768]{1,0:T(8,128)(2,1)S(1)}, bf16[64,768]{1,0:T(8,128)(2,1)S(1)}, u32[]{:S(2)}, u32[]{:S(2)}) collective-permute-start(bf16[64,768]{1,0:T(8,128)(2,1)S(1)} %collective-permute-done.12.refs_5_), channel_id=1, source_target_pairs={{0,129},{8,137},{16,145},{24,153},{32,161},{40,169},{48,177},{56,1... | collective-permute-start | bytes 294920 | tf_op jit(solution)/shard_map/ppermute | solution.py:37
  36.0 1.2 shard_map.62
  37.2 0.2 select_reduce_fusion
  37.4 2.0 %shard_map.63 = (bf16[768,512]{1,0:T(8,128)(2,1)S(1)}, bf16[768,512]{1,0:T(8,128)(2,1)S(1)}, bf16[512,768]{1,0:T(8,128)(2,1)S(1)}, f32[2,4,128]{2,1,0:T(4,128)S(1)}) custom-call(bf16[768,768]{1,0:T(8,128)(2,1)S(1)} %copy-done, bf16[768,768]{1,0:T(8,128)(2,1)S(1)} %collective-permute-done.refs_1_, f32[768,1]{1,0:T(8,128)S(1)} %mul.128.refs_2_, ...), custom_call_target="tpu_custom_call" | custom-call | flops 1207959552 | bytes 3932160 | tf_op jit(solution)/shard_map/pallas_call | solution.py:81
  39.5 1.2 shard_map.64
  40.6 0.6 shard_map.65.near
  41.2 2.6 %collective-permute-start.15 = (f32[3,8,128]{2,1,0:T(8,128)S(1)}, f32[3,8,128]{2,1,0:T(8,128)S(1)}, u32[]{:S(2)}, u32[]{:S(2)}) collective-permute-start(f32[3,8,128]{2,1,0:T(8,128)S(1)} %get-tuple-element.123), channel_id=1, source_target_pairs={{0,129},{8,137},{16,145},{24,153},{32,161},{40,169},{48,177},{56,1... | collective-permute-start | bytes 36872 | tf_op jit(solution)/shard_map/ppermute | solution.py:37
  43.9 0.8 collective-permute-done.15
  44.7 2.9 %collective-permute-done.16 = f32[3,8,128]{2,1,0:T(8,128)S(1)} collective-permute-done((f32[3,8,128]{2,1,0:T(8,128)S(1)}, f32[3,8,128]{2,1,0:T(8,128)S(1)}, u32[]{:S(2)}, u32[]{:S(2)}) %collective-permute-start.16) | collective-permute-done | bytes 12320 | tf_op jit(solution)/shard_map/ppermute | solution.py:37
  47.7 13.0 %all_to_all.15.parts = f32[8,3,2,8,128]{4,3,2,1,0:T(8,128)S(1)} all-to-all(f32[8,3,2,8,128]{4,3,2,1,0:T(8,128)S(1)} %broadcast_in_dim.20), channel_id=1, replica_groups={{0,16,32,48,64,80,96,112},{8,24,40,56,72,88,104,120},{128,144,160,176,1..., dimensions={0} | all-to-all | bytes 393216 | tf_op jit(solution)/shard_map/all_to_all | solution.py:334
  60.8 3.7 %shard_map.67 = (f32[8,104,768]{2,1,0:T(8,128)S(1)}, f32[8,128]{1,0:T(8,128)S(1)}) custom-call(s32[2]{0:T(128)S(1)} %get-tuple-element.90.position, f32[3,2,8,128]{3,2,1,0:T(8,128)S(1)} %shard_map.65.near, f32[8,3,2,8,128]{4,3,2,1,0:T(8,128)S(1)} %all_to_all.15.parts, bf16[768,256]{1,0:T(8,128)(2,1)S(1)} %get-tuple-element.81.refs_0_, ...), custom_call_target="tpu_custom_call" | custom-call | flops 2617245696 | bytes 6291456 | tf_op jit(solution)/shard_map/pallas_call | solution.py:194
  64.5 8.1 %collective-permute-start.17 = (f32[8,104,768]{2,1,0:T(8,128)S(1)}, f32[8,104,768]{2,1,0:T(8,128)S(1)}, u32[]{:S(2)}, u32[]{:S(2)}) collective-permute-start(f32[8,104,768]{2,1,0:T(8,128)S(1)} %get-tuple-element.87), channel_id=1, source_target_pairs={{0,8},{8,0},{16,24},{24,16},{32,40},{40,32},{48,56},{56,48},{64,72... | collective-permute-start | bytes 7667720 | tf_op jit(solution)/shard_map/ppermute | solution.py:37
  72.6 3.7 %shard_map.66 = (f32[8,104,768]{2,1,0:T(8,128)S(1)}, f32[8,128]{1,0:T(8,128)S(1)}) custom-call(s32[2]{0:T(128)S(1)} %get-tuple-element.91.position, f32[3,2,8,128]{3,2,1,0:T(8,128)S(1)} %shard_map.65.near, f32[8,3,2,8,128]{4,3,2,1,0:T(8,128)S(1)} %all_to_all.15.parts, bf16[768,256]{1,0:T(8,128)(2,1)S(1)} %get-tuple-element.68.refs_0_, ...), custom_call_target="tpu_custom_call" | custom-call | flops 2617245696 | bytes 6291456 | tf_op jit(solution)/shard_map/pallas_call | solution.py:194
  76.3 0.6 collective-permute-done.18.taken_counts
  77.0 0.6 shard_map.68
  77.5 1.2 convert_element_type.76
  78.8 4.0 %all-to-all-start.1 = ((f16[8,627,128]{2,1,0:T(8,128)(2,1)}), f16[8,627,128]{2,1,0:T(8,128)(2,1)S(1)}, u32[]{:S(2)}, u32[]{:S(2)}) async-start(f16[8,627,128]{2,1,0:T(8,128)(2,1)} %convert_element_type.76), calls=%async_computation.1 | async-start | bytes 2588672 | tf_op jit(solution)/shard_map/all_to_all | solution.py:344
  82.8 19.5 %all-to-all-done.1 = f16[8,627,128]{2,1,0:T(8,128)(2,1)S(1)} async-done(((f16[8,627,128]{2,1,0:T(8,128)(2,1)}), f16[8,627,128]{2,1,0:T(8,128)(2,1)S(1)}, u32[]{:S(2)}, u32[]{:S(2)}) %all-to-all-start.1) | async-done | bytes 1284128 | tf_op jit(solution)/shard_map/all_to_all | solution.py:344
  102.5 0.8 multiply_reduce_fusion
  103.7 0.2 fusion.1
  104.0 0.2 broadcast_in_dim.22
  104.1 20.8 %all_to_all.16 = f16[8,625,128]{2,1,0:T(8,128)(2,1)S(1)} all-to-all(f16[8,625,128]{2,1,0:T(8,128)(2,1)S(1)} %broadcast_in_dim.22), channel_id=1, replica_groups=mesh['blk'=32,'dp'=8] {'dp'}, dimensions={0} | all-to-all | bytes 2560000 | tf_op jit(solution)/shard_map/all_to_all | solution.py:371
  125.0 0.2 slice.245
  125.3 0.2 fusion.17
  125.9 0.8 convert_multiply_fusion.1
  127.0 1.9 %convert_multiply_fusion = f32[768,768]{1,0:T(8,128)} fusion(f16[768,768]{1,0:T(8,128)(2,1)S(1)} %constant_dynamic-update-slice_fusion, f32[768]{0:T(1024)S(1)} %mul.122), kind=kLoop, calls=%fused_computation.4 | loop fusion | flops 1179648 | bytes 3542016 | tf_op jit(solution)/shard_map/mul | solution.py:378
  (77 shorter events, 1.9 us)
Async XLA Ops:
  0.6 9.4 %copy-start.1 = (bf16[128,768]{1,0:T(8,128)(2,1)S(1)}, bf16[128,768]{1,0:T(8,128)(2,1)}, u32[]{:S(2)}) copy-start(bf16[128,768]{1,0:T(8,128)(2,1)} %refs_4_.1) | copy-start | bytes 589828
  0.6 11.3 %collective-permute-start.1 = (bf16[128,768]{1,0:T(8,128)(2,1)}, bf16[128,768]{1,0:T(8,128)(2,1)S(1)}, u32[]{:S(2)}, u32[]{:S(2)}) collective-permute-start(bf16[128,768]{1,0:T(8,128)(2,1)} %refs_4_.1), channel_id=1, source_target_pairs={{0,16},{8,24},{16,32},{24,40},{32,48},{40,56},{48,64},{56,72},{64,... | collective-permute-start | bytes 589832 | tf_op jit(solution)/shard_map/ppermute | solution.py:37
  3.2 8.8 %collective-permute-start.2 = (bf16[128,768]{1,0:T(8,128)(2,1)}, bf16[128,768]{1,0:T(8,128)(2,1)S(1)}, u32[]{:S(2)}, u32[]{:S(2)}) collective-permute-start(bf16[128,768]{1,0:T(8,128)(2,1)} %refs_4_.1), channel_id=1, source_target_pairs={{0,112},{8,120},{16,0},{24,8},{32,16},{40,24},{48,32},{56,40},{64,... | collective-permute-start | bytes 589832 | tf_op jit(solution)/shard_map/ppermute | solution.py:37
  7.2 7.5 %collective-permute-start = (bf16[768,768]{1,0:T(8,128)(2,1)}, bf16[768,768]{1,0:T(8,128)(2,1)S(1)}, u32[]{:S(2)}, u32[]{:S(2)}) collective-permute-start(bf16[768,768]{1,0:T(8,128)(2,1)} %refs_0_.11), channel_id=1, source_target_pairs={{0,8},{8,0},{16,24},{24,16},{32,40},{40,32},{48,56},{56,48},{64,72... | collective-permute-start | bytes 3538952 | tf_op jit(solution)/shard_map/ppermute | solution.py:37
  12.0 6.4 %collective-permute-start.5 = (bf16[128,768]{1,0:T(8,128)(2,1)S(1)}, bf16[128,768]{1,0:T(8,128)(2,1)S(1)}, u32[]{:S(2)}, u32[]{:S(2)}) collective-permute-start(bf16[128,768]{1,0:T(8,128)(2,1)S(1)} %collective-permute-done.1.refs_4_), channel_id=1, source_target_pairs={{0,16},{8,24},{16,32},{24,40},{32,48},{40,56},{48,64},{56,72},{64,... | collective-permute-start | bytes 589832 | tf_op jit(solution)/shard_map/ppermute | solution.py:37
  12.0 6.4 %collective-permute-start.6 = (bf16[128,768]{1,0:T(8,128)(2,1)S(1)}, bf16[128,768]{1,0:T(8,128)(2,1)S(1)}, u32[]{:S(2)}, u32[]{:S(2)}) collective-permute-start(bf16[128,768]{1,0:T(8,128)(2,1)S(1)} %collective-permute-done.2.refs_5_), channel_id=1, source_target_pairs={{0,112},{8,120},{16,0},{24,8},{32,16},{40,24},{48,32},{56,40},{64,... | collective-permute-start | bytes 589832 | tf_op jit(solution)/shard_map/ppermute | solution.py:37
  14.7 1.3 copy-start
  18.3 6.6 %collective-permute-start.7 = (bf16[128,768]{1,0:T(8,128)(2,1)S(1)}, bf16[128,768]{1,0:T(8,128)(2,1)S(1)}, u32[]{:S(2)}, u32[]{:S(2)}) collective-permute-start(bf16[128,768]{1,0:T(8,128)(2,1)S(1)} %collective-permute-done.5.refs_4_), channel_id=1, source_target_pairs={{0,16},{8,24},{16,32},{24,40},{32,48},{40,56},{48,64},{56,72},{64,... | collective-permute-start | bytes 589832 | tf_op jit(solution)/shard_map/ppermute | solution.py:37
  18.3 6.6 %collective-permute-start.8 = (bf16[128,768]{1,0:T(8,128)(2,1)S(1)}, bf16[128,768]{1,0:T(8,128)(2,1)S(1)}, u32[]{:S(2)}, u32[]{:S(2)}) collective-permute-start(bf16[128,768]{1,0:T(8,128)(2,1)S(1)} %collective-permute-done.6.refs_5_), channel_id=1, source_target_pairs={{0,112},{8,120},{16,0},{24,8},{32,16},{40,24},{48,32},{56,40},{64,... | collective-permute-start | bytes 589832 | tf_op jit(solution)/shard_map/ppermute | solution.py:37
  21.0 7.4 %collective-permute-start.3 = (bf16[192,768]{1,0:T(8,128)(2,1)S(1)}, bf16[192,768]{1,0:T(8,128)(2,1)S(1)}, u32[]{:S(2)}, u32[]{:S(2)}) collective-permute-start(bf16[192,768]{1,0:T(8,128)(2,1)S(1)} %get-tuple-element.47), channel_id=1, source_target_pairs={{0,128},{8,136},{16,144},{24,152},{32,160},{40,168},{48,176},{56,1... | collective-permute-start | bytes 884744 | tf_op jit(solution)/shard_map/ppermute | solution.py:37
  22.3 8.4 %collective-permute-start.4 = (bf16[192,768]{1,0:T(8,128)(2,1)S(1)}, bf16[192,768]{1,0:T(8,128)(2,1)S(1)}, u32[]{:S(2)}, u32[]{:S(2)}) collective-permute-start(bf16[192,768]{1,0:T(8,128)(2,1)S(1)} %get-tuple-element.48), channel_id=1, source_target_pairs={{0,129},{8,137},{16,145},{24,153},{32,161},{40,169},{48,177},{56,1... | collective-permute-start | bytes 884744 | tf_op jit(solution)/shard_map/ppermute | solution.py:37
  25.0 7.7 %collective-permute-start.11 = (bf16[64,768]{1,0:T(8,128)(2,1)S(1)}, bf16[64,768]{1,0:T(8,128)(2,1)S(1)}, u32[]{:S(2)}, u32[]{:S(2)}) collective-permute-start(bf16[64,768]{1,0:T(8,128)(2,1)S(1)} %get-tuple-element.109), channel_id=1, source_target_pairs={{0,16},{8,24},{16,32},{24,40},{32,48},{40,56},{48,64},{56,72},{64,... | collective-permute-start | bytes 294920 | tf_op jit(solution)/shard_map/ppermute | solution.py:37
  25.6 7.1 %collective-permute-start.12 = (bf16[64,768]{1,0:T(8,128)(2,1)S(1)}, bf16[64,768]{1,0:T(8,128)(2,1)S(1)}, u32[]{:S(2)}, u32[]{:S(2)}) collective-permute-start(bf16[64,768]{1,0:T(8,128)(2,1)S(1)} %get-tuple-element.110), channel_id=1, source_target_pairs={{0,112},{8,120},{16,0},{24,8},{32,16},{40,24},{48,32},{56,40},{64,... | collective-permute-start | bytes 294920 | tf_op jit(solution)/shard_map/ppermute | solution.py:37
  27.9 4.8 %copy-start.2 = (s32[1024]{0:T(1024)S(1)}, s32[1024]{0:T(1024)}, u32[]{:S(2)}) copy-start(s32[1024]{0:T(1024)} %param.7) | copy-start | bytes 12292
  27.9 9.5 %collective-permute-start.9 = (bf16[256,768]{1,0:T(8,128)(2,1)S(1)}, bf16[256,768]{1,0:T(8,128)(2,1)S(1)}, u32[]{:S(2)}, u32[]{:S(2)}) collective-permute-start(bf16[256,768]{1,0:T(8,128)(2,1)S(1)} %pad_maximum_fusion), channel_id=1, source_target_pairs={{0,128},{8,136},{16,144},{24,152},{32,160},{40,168},{48,176},{56,1... | collective-permute-start | bytes 1179656 | tf_op jit(solution)/shard_map/ppermute | solution.py:37
  28.4 9.0 %collective-permute-start.10 = (bf16[256,768]{1,0:T(8,128)(2,1)S(1)}, bf16[256,768]{1,0:T(8,128)(2,1)S(1)}, u32[]{:S(2)}, u32[]{:S(2)}) collective-permute-start(bf16[256,768]{1,0:T(8,128)(2,1)S(1)} %pad_maximum_fusion.1), channel_id=1, source_target_pairs={{0,129},{8,137},{16,145},{24,153},{32,161},{40,169},{48,177},{56,1... | collective-permute-start | bytes 1179656 | tf_op jit(solution)/shard_map/ppermute | solution.py:37
  33.3 3.9 %copy-start.3 = (s32[128]{0:T(128)S(1)}, s32[128]{0:T(128)}, u32[]{:S(2)}) copy-start(s32[128]{0:T(128)} %param.6) | copy-start | bytes 1540
  33.3 6.2 %collective-permute-start.13 = (bf16[64,768]{1,0:T(8,128)(2,1)S(1)}, bf16[64,768]{1,0:T(8,128)(2,1)S(1)}, u32[]{:S(2)}, u32[]{:S(2)}) collective-permute-start(bf16[64,768]{1,0:T(8,128)(2,1)S(1)} %collective-permute-done.11.refs_4_), channel_id=1, source_target_pairs={{0,128},{8,136},{16,144},{24,152},{32,160},{40,168},{48,176},{56,1... | collective-permute-start | bytes 294920 | tf_op jit(solution)/shard_map/ppermute | solution.py:37
  33.4 6.1 %collective-permute-start.14 = (bf16[64,768]{1,0:T(8,128)(2,1)S(1)}, bf16[64,768]{1,0:T(8,128)(2,1)S(1)}, u32[]{:S(2)}, u32[]{:S(2)}) collective-permute-start(bf16[64,768]{1,0:T(8,128)(2,1)S(1)} %collective-permute-done.12.refs_5_), channel_id=1, source_target_pairs={{0,129},{8,137},{16,145},{24,153},{32,161},{40,169},{48,177},{56,1... | collective-permute-start | bytes 294920 | tf_op jit(solution)/shard_map/ppermute | solution.py:37
  41.2 3.5 %collective-permute-start.15 = (f32[3,8,128]{2,1,0:T(8,128)S(1)}, f32[3,8,128]{2,1,0:T(8,128)S(1)}, u32[]{:S(2)}, u32[]{:S(2)}) collective-permute-start(f32[3,8,128]{2,1,0:T(8,128)S(1)} %get-tuple-element.123), channel_id=1, source_target_pairs={{0,129},{8,137},{16,145},{24,153},{32,161},{40,169},{48,177},{56,1... | collective-permute-start | bytes 36872 | tf_op jit(solution)/shard_map/ppermute | solution.py:37
  43.9 3.8 %collective-permute-start.16 = (f32[3,8,128]{2,1,0:T(8,128)S(1)}, f32[3,8,128]{2,1,0:T(8,128)S(1)}, u32[]{:S(2)}, u32[]{:S(2)}) collective-permute-start(f32[3,8,128]{2,1,0:T(8,128)S(1)} %get-tuple-element.124), channel_id=1, source_target_pairs={{0,128},{8,136},{16,144},{24,152},{32,160},{40,168},{48,176},{56,1... | collective-permute-start | bytes 36872 | tf_op jit(solution)/shard_map/ppermute | solution.py:37
  64.5 12.5 %collective-permute-start.17 = (f32[8,104,768]{2,1,0:T(8,128)S(1)}, f32[8,104,768]{2,1,0:T(8,128)S(1)}, u32[]{:S(2)}, u32[]{:S(2)}) collective-permute-start(f32[8,104,768]{2,1,0:T(8,128)S(1)} %get-tuple-element.87), channel_id=1, source_target_pairs={{0,8},{8,0},{16,24},{24,16},{32,40},{40,32},{48,56},{56,48},{64,72... | collective-permute-start | bytes 7667720 | tf_op jit(solution)/shard_map/ppermute | solution.py:37
  72.5 4.4 %collective-permute-start.18 = (f32[8,128]{1,0:T(8,128)S(1)}, f32[8,128]{1,0:T(8,128)S(1)}, u32[]{:S(2)}, u32[]{:S(2)}) collective-permute-start(f32[8,128]{1,0:T(8,128)S(1)} %get-tuple-element.89), channel_id=1, source_target_pairs={{0,8},{8,0},{16,24},{24,16},{32,40},{40,32},{48,56},{56,48},{64,72... | collective-permute-start | bytes 12296 | tf_op jit(solution)/shard_map/ppermute | solution.py:37
  78.8 23.5 %all-to-all-start.1 = ((f16[8,627,128]{2,1,0:T(8,128)(2,1)}), f16[8,627,128]{2,1,0:T(8,128)(2,1)S(1)}, u32[]{:S(2)}, u32[]{:S(2)}) async-start(f16[8,627,128]{2,1,0:T(8,128)(2,1)} %convert_element_type.76), calls=%async_computation.1 | async-start | bytes 2588672 | tf_op jit(solution)/shard_map/all_to_all | solution.py:344

commit v4 on v3

--- a/solution.py
+++ b/solution.py
@@ -48,7 +48,7 @@
     n = rows.shape[0]
     for s, a, m, b in plan:
         rows[b : b + m, :] = sources[s][a : a + m, :]
-    factor = 2.0 / math.sqrt(width)
+    factor = 2.0 / math.sqrt(width) * math.log2(math.e)
     for at in range(0, n, TILE):
         m = min(TILE, n - at)
         block = rows[at : at + m, :]
@@ -65,7 +65,7 @@
         top = jnp.maximum(*(jnp.max(part, axis=0, keepdims=True) for part in scores))
         total = jnp.zeros((1, m), jnp.float32)
         for part, expo in zip(scores, expos):
-            value = jnp.exp(part - top)
+            value = jnp.exp2(part - top)
             total += jnp.sum(value, axis=0, keepdims=True)
             expo[:, at : at + m] = value.astype(jnp.bfloat16)
         for j in range(0, m, LANES):
@@ -142,8 +142,8 @@
     ratio, number = [], []
     for i in range(2):
         top = functools.reduce(jnp.maximum, [parts[j, 0, i] for j in range(Z)])
-        whole = sum(parts[j, 1, i] * jnp.exp(parts[j, 0, i] - top) for j in range(Z))
-        ratio.append(jnp.exp(near[0, i] - top) / whole)
+        whole = sum(parts[j, 1, i] * jnp.exp2(parts[j, 0, i] - top) for j in range(Z))
+        ratio.append(jnp.exp2(near[0, i] - top) / whole)
         number.append(sum(parts[j, 2, i] for j in range(Z)))
     scale[0], scale[1] = unfolded(ratio)
     slot[0], slot[1] = unfolded(number)
@@ -247,7 +247,7 @@
 
 def combine(first, second):
     top = jnp.maximum(first[0], second[0])
-    total = first[1] * jnp.exp(first[0] - top) + second[1] * jnp.exp(second[0] - top)
+    total = first[1] * jnp.exp2(first[0] - top) + second[1] * jnp.exp2(second[0] - top)
     return jnp.stack([top, total, first[2] + second[2]])
 
 

time: 129 us -> 129 us (level)
  transfers between devices with their start and end apart: 20 -> 20, of which waited for: 6 -> 6; matrix products, arithmetic and copies ran while one was open for 2% -> 2% of each run, Pallas kernels for 9% -> 8%
where the time goes in v4:
time: 129 us
  starting transfers between devices  39.1 us (30%)
  blocking collectives  33.9 us (26%)
  waiting for transfers between devices  27.2 us (21%)
  Pallas kernels  16.8 us (13%)
  other arithmetic  8.12 us (6%)
  local copies, waits for them, and re-layouts  2.71 us (2%)
    ppermute x19, starting transfers between devices, shifted(): return lax.ppermute(value, AXES, pairs)  35.1 us
    all_to_all x1, blocking collectives, local(): lax.all_to_all(jnp.broadcast_to(sent[None], (PEERS, *sent.shape)), 'dp',...  20.8 us
    all_to_all x1, waiting for transfers between devices, local(): lax.all_to_all(packed_sums(kept, taken).astype(jnp.float16), 'dp', split_...  19.5 us
    all_to_all x1, blocking collectives, local(): lax.all_to_all(jnp.broadcast_to(stats[None], (Z, *stats.shape)), 'blk', 0...  13 us
    pallas_call x6, Pallas kernels, score_rows(): pl.pallas_call(functools.partial(score_kernel, plan, len(sources)), in_sp...  8.32 us
    ppermute x19, waiting for transfers between devices, shifted(): return lax.ppermute(value, AXES, pairs)  7.67 us
    pallas_call x2, Pallas kernels, sum_rows(): pl.pallas_call(functools.partial(sum_kernel, groups, sizes), in_specs=[pl...  7.36 us
    all_to_all x1, starting transfers between devices, local(): lax.all_to_all(packed_sums(kept, taken).astype(jnp.float16), 'dp', split_...  4.01 us
  transfers between devices with their start and end apart: 20, of which 6 were waited for; matrix products, arithmetic and copies ran while one was open for 2% of the time, Pallas kernels for 8%

profile of v4, /device:TPU:1, one launch (start us, length us, event | category | flops | bytes accessed | tf_op | source)
XLA Modules:
  0.0 128.9 jit_solution(18422477664093177854)
XLA Ops:
  0.6 2.5 %collective-permute-start.1 = (bf16[128,768]{1,0:T(8,128)(2,1)}, bf16[128,768]{1,0:T(8,128)(2,1)S(1)}, u32[]{:S(2)}, u32[]{:S(2)}) collective-permute-start(bf16[128,768]{1,0:T(8,128)(2,1)} %refs_4_.1), channel_id=1, source_target_pairs={{0,16},{8,24},{16,32},{24,40},{32,48},{40,56},{48,64},{56,72},{64,... | collective-permute-start | bytes 589832 | tf_op jit(solution)/shard_map/ppermute | solution.py:37
  3.2 4.0 %collective-permute-start.2 = (bf16[128,768]{1,0:T(8,128)(2,1)}, bf16[128,768]{1,0:T(8,128)(2,1)S(1)}, u32[]{:S(2)}, u32[]{:S(2)}) collective-permute-start(bf16[128,768]{1,0:T(8,128)(2,1)} %refs_4_.1), channel_id=1, source_target_pairs={{0,112},{8,120},{16,0},{24,8},{32,16},{40,24},{48,32},{56,40},{64,... | collective-permute-start | bytes 589832 | tf_op jit(solution)/shard_map/ppermute | solution.py:37
  7.2 1.0 collective-permute-start
  8.2 1.6 %multiply_reduce_fusion.2 = f32[768]{0:T(1024)S(1)} fusion(bf16[768,768]{1,0:T(8,128)(2,1)} %refs_0_.11), kind=kLoop, calls=%fused_computation.6 | loop fusion | flops 1768704 | bytes 1182720 | tf_op jit(solution)/shard_map/reduce_sum | solution.py:277
  9.8 0.2 mul.128.refs_2_
  10.1 1.9 %collective-permute-done.1.refs_4_ = bf16[128,768]{1,0:T(8,128)(2,1)S(1)} collective-permute-done((bf16[128,768]{1,0:T(8,128)(2,1)}, bf16[128,768]{1,0:T(8,128)(2,1)S(1)}, u32[]{:S(2)}, u32[]{:S(2)}) %collective-permute-start.1) | collective-permute-done | bytes 196640 | tf_op jit(solution)/shard_map/ppermute | solution.py:37
  12.0 2.7 %collective-permute-start.6 = (bf16[128,768]{1,0:T(8,128)(2,1)S(1)}, bf16[128,768]{1,0:T(8,128)(2,1)S(1)}, u32[]{:S(2)}, u32[]{:S(2)}) collective-permute-start(bf16[128,768]{1,0:T(8,128)(2,1)S(1)} %collective-permute-done.2.refs_5_), channel_id=1, source_target_pairs={{0,112},{8,120},{16,0},{24,8},{32,16},{40,24},{48,32},{56,40},{64,... | collective-permute-start | bytes 589832 | tf_op jit(solution)/shard_map/ppermute | solution.py:37
  14.8 0.3 multiply_reduce_fusion.1
  15.1 0.2 mul.129.refs_3_
  15.2 0.7 copy-done
  16.0 1.1 shard_map.59
  17.1 1.3 collective-permute-done.5.refs_4_
  18.3 2.7 %collective-permute-start.8 = (bf16[128,768]{1,0:T(8,128)(2,1)S(1)}, bf16[128,768]{1,0:T(8,128)(2,1)S(1)}, u32[]{:S(2)}, u32[]{:S(2)}) collective-permute-start(bf16[128,768]{1,0:T(8,128)(2,1)S(1)} %collective-permute-done.6.refs_5_), channel_id=1, source_target_pairs={{0,112},{8,120},{16,0},{24,8},{32,16},{40,24},{48,32},{56,40},{64,... | collective-permute-start | bytes 589832 | tf_op jit(solution)/shard_map/ppermute | solution.py:37
  21.0 1.3 %collective-permute-start.3 = (bf16[192,768]{1,0:T(8,128)(2,1)S(1)}, bf16[192,768]{1,0:T(8,128)(2,1)S(1)}, u32[]{:S(2)}, u32[]{:S(2)}) collective-permute-start(bf16[192,768]{1,0:T(8,128)(2,1)S(1)} %get-tuple-element.47), channel_id=1, source_target_pairs={{0,128},{8,136},{16,144},{24,152},{32,160},{40,168},{48,176},{56,1... | collective-permute-start | bytes 884744 | tf_op jit(solution)/shard_map/ppermute | solution.py:37
  22.3 1.4 %collective-permute-start.4 = (bf16[192,768]{1,0:T(8,128)(2,1)S(1)}, bf16[192,768]{1,0:T(8,128)(2,1)S(1)}, u32[]{:S(2)}, u32[]{:S(2)}) collective-permute-start(bf16[192,768]{1,0:T(8,128)(2,1)S(1)} %get-tuple-element.48), channel_id=1, source_target_pairs={{0,129},{8,137},{16,145},{24,153},{32,161},{40,169},{48,177},{56,1... | collective-permute-start | bytes 884744 | tf_op jit(solution)/shard_map/ppermute | solution.py:37
  23.8 1.1 shard_map.61
  24.9 0.7 collective-permute-start.11
  25.6 2.2 %collective-permute-start.12 = (bf16[64,768]{1,0:T(8,128)(2,1)S(1)}, bf16[64,768]{1,0:T(8,128)(2,1)S(1)}, u32[]{:S(2)}, u32[]{:S(2)}) collective-permute-start(bf16[64,768]{1,0:T(8,128)(2,1)S(1)} %get-tuple-element.110), channel_id=1, source_target_pairs={{0,112},{8,120},{16,0},{24,8},{32,16},{40,24},{48,32},{56,40},{64,... | collective-permute-start | bytes 294920 | tf_op jit(solution)/shard_map/ppermute | solution.py:37
  27.9 0.5 collective-permute-start.9
  28.4 2.2 %collective-permute-start.10 = (bf16[256,768]{1,0:T(8,128)(2,1)S(1)}, bf16[256,768]{1,0:T(8,128)(2,1)S(1)}, u32[]{:S(2)}, u32[]{:S(2)}) collective-permute-start(bf16[256,768]{1,0:T(8,128)(2,1)S(1)} %pad_maximum_fusion.1), channel_id=1, source_target_pairs={{0,129},{8,137},{16,145},{24,153},{32,161},{40,169},{48,177},{56,1... | collective-permute-start | bytes 1179656 | tf_op jit(solution)/shard_map/ppermute | solution.py:37
  30.6 1.9 %shard_map.60 = (bf16[768,512]{1,0:T(8,128)(2,1)S(1)}, bf16[768,512]{1,0:T(8,128)(2,1)S(1)}, bf16[512,768]{1,0:T(8,128)(2,1)S(1)}, f32[2,4,128]{2,1,0:T(4,128)S(1)}) custom-call(bf16[768,768]{1,0:T(8,128)(2,1)S(1)} %copy-done, bf16[768,768]{1,0:T(8,128)(2,1)S(1)} %collective-permute-done.refs_1_, f32[768,1]{1,0:T(8,128)S(1)} %mul.128.refs_2_, ...), custom_call_target="tpu_custom_call" | custom-call | flops 1207959552 | bytes 3932160 | tf_op jit(solution)/shard_map/pallas_call | solution.py:81
  32.6 0.5 convert_reduce_fusion
  33.2 2.7 %collective-permute-start.14 = (bf16[64,768]{1,0:T(8,128)(2,1)S(1)}, bf16[64,768]{1,0:T(8,128)(2,1)S(1)}, u32[]{:S(2)}, u32[]{:S(2)}) collective-permute-start(bf16[64,768]{1,0:T(8,128)(2,1)S(1)} %collective-permute-done.12.refs_5_), channel_id=1, source_target_pairs={{0,129},{8,137},{16,145},{24,153},{32,161},{40,169},{48,177},{56,1... | collective-permute-start | bytes 294920 | tf_op jit(solution)/shard_map/ppermute | solution.py:37
  35.9 1.1 shard_map.62
  37.0 0.2 select_reduce_fusion
  37.2 1.9 %shard_map.63 = (bf16[768,512]{1,0:T(8,128)(2,1)S(1)}, bf16[768,512]{1,0:T(8,128)(2,1)S(1)}, bf16[512,768]{1,0:T(8,128)(2,1)S(1)}, f32[2,4,128]{2,1,0:T(4,128)S(1)}) custom-call(bf16[768,768]{1,0:T(8,128)(2,1)S(1)} %copy-done, bf16[768,768]{1,0:T(8,128)(2,1)S(1)} %collective-permute-done.refs_1_, f32[768,1]{1,0:T(8,128)S(1)} %mul.128.refs_2_, ...), custom_call_target="tpu_custom_call" | custom-call | flops 1207959552 | bytes 3932160 | tf_op jit(solution)/shard_map/pallas_call | solution.py:81
  39.3 1.1 shard_map.64
  40.4 0.6 shard_map.65.near
  41.0 2.7 %collective-permute-start.15 = (f32[3,8,128]{2,1,0:T(8,128)S(1)}, f32[3,8,128]{2,1,0:T(8,128)S(1)}, u32[]{:S(2)}, u32[]{:S(2)}) collective-permute-start(f32[3,8,128]{2,1,0:T(8,128)S(1)} %get-tuple-element.123), channel_id=1, source_target_pairs={{0,129},{8,137},{16,145},{24,153},{32,161},{40,169},{48,177},{56,1... | collective-permute-start | bytes 36872 | tf_op jit(solution)/shard_map/ppermute | solution.py:37
  43.7 0.8 collective-permute-done.15
  44.5 2.9 %collective-permute-done.16 = f32[3,8,128]{2,1,0:T(8,128)S(1)} collective-permute-done((f32[3,8,128]{2,1,0:T(8,128)S(1)}, f32[3,8,128]{2,1,0:T(8,128)S(1)}, u32[]{:S(2)}, u32[]{:S(2)}) %collective-permute-start.16) | collective-permute-done | bytes 12320 | tf_op jit(solution)/shard_map/ppermute | solution.py:37
  47.5 13.0 %all_to_all.15.parts = f32[8,3,2,8,128]{4,3,2,1,0:T(8,128)S(1)} all-to-all(f32[8,3,2,8,128]{4,3,2,1,0:T(8,128)S(1)} %broadcast_in_dim.20), channel_id=1, replica_groups={{0,16,32,48,64,80,96,112},{8,24,40,56,72,88,104,120},{128,144,160,176,1..., dimensions={0} | all-to-all | bytes 393216 | tf_op jit(solution)/shard_map/all_to_all | solution.py:334
  60.5 3.7 %shard_map.67 = (f32[8,104,768]{2,1,0:T(8,128)S(1)}, f32[8,128]{1,0:T(8,128)S(1)}) custom-call(s32[2]{0:T(128)S(1)} %get-tuple-element.90.position, f32[3,2,8,128]{3,2,1,0:T(8,128)S(1)} %shard_map.65.near, f32[8,3,2,8,128]{4,3,2,1,0:T(8,128)S(1)} %all_to_all.15.parts, bf16[768,256]{1,0:T(8,128)(2,1)S(1)} %get-tuple-element.81.refs_0_, ...), custom_call_target="tpu_custom_call" | custom-call | flops 2617245696 | bytes 6291456 | tf_op jit(solution)/shard_map/pallas_call | solution.py:194
  64.2 8.3 %collective-permute-start.17 = (f32[8,104,768]{2,1,0:T(8,128)S(1)}, f32[8,104,768]{2,1,0:T(8,128)S(1)}, u32[]{:S(2)}, u32[]{:S(2)}) collective-permute-start(f32[8,104,768]{2,1,0:T(8,128)S(1)} %get-tuple-element.87), channel_id=1, source_target_pairs={{0,8},{8,0},{16,24},{24,16},{32,40},{40,32},{48,56},{56,48},{64,72... | collective-permute-start | bytes 7667720 | tf_op jit(solution)/shard_map/ppermute | solution.py:37
  72.6 3.7 %shard_map.66 = (f32[8,104,768]{2,1,0:T(8,128)S(1)}, f32[8,128]{1,0:T(8,128)S(1)}) custom-call(s32[2]{0:T(128)S(1)} %get-tuple-element.91.position, f32[3,2,8,128]{3,2,1,0:T(8,128)S(1)} %shard_map.65.near, f32[8,3,2,8,128]{4,3,2,1,0:T(8,128)S(1)} %all_to_all.15.parts, bf16[768,256]{1,0:T(8,128)(2,1)S(1)} %get-tuple-element.68.refs_0_, ...), custom_call_target="tpu_custom_call" | custom-call | flops 2617245696 | bytes 6291456 | tf_op jit(solution)/shard_map/pallas_call | solution.py:194
  76.3 0.7 collective-permute-done.18.taken_counts
  77.0 0.6 shard_map.68
  77.6 1.2 convert_element_type.76
  78.8 4.0 %all-to-all-start.1 = ((f16[8,627,128]{2,1,0:T(8,128)(2,1)}), f16[8,627,128]{2,1,0:T(8,128)(2,1)S(1)}, u32[]{:S(2)}, u32[]{:S(2)}) async-start(f16[8,627,128]{2,1,0:T(8,128)(2,1)} %convert_element_type.76), calls=%async_computation.1 | async-start | bytes 2588672 | tf_op jit(solution)/shard_map/all_to_all | solution.py:344
  82.8 19.5 %all-to-all-done.1 = f16[8,627,128]{2,1,0:T(8,128)(2,1)S(1)} async-done(((f16[8,627,128]{2,1,0:T(8,128)(2,1)}), f16[8,627,128]{2,1,0:T(8,128)(2,1)S(1)}, u32[]{:S(2)}, u32[]{:S(2)}) %all-to-all-start.1) | async-done | bytes 1284128 | tf_op jit(solution)/shard_map/all_to_all | solution.py:344
  102.5 0.8 multiply_reduce_fusion
  103.7 0.2 fusion.1
  104.0 0.2 broadcast_in_dim.22
  104.1 20.8 %all_to_all.16 = f16[8,625,128]{2,1,0:T(8,128)(2,1)S(1)} all-to-all(f16[8,625,128]{2,1,0:T(8,128)(2,1)S(1)} %broadcast_in_dim.22), channel_id=1, replica_groups=mesh['blk'=32,'dp'=8] {'dp'}, dimensions={0} | all-to-all | bytes 2560000 | tf_op jit(solution)/shard_map/all_to_all | solution.py:371
  125.0 0.2 slice.245
  125.3 0.2 fusion.17
  125.9 0.8 convert_multiply_fusion.1
  127.0 1.9 %convert_multiply_fusion = f32[768,768]{1,0:T(8,128)} fusion(f16[768,768]{1,0:T(8,128)(2,1)S(1)} %constant_dynamic-update-slice_fusion, f32[768]{0:T(1024)S(1)} %mul.122), kind=kLoop, calls=%fused_computation.4 | loop fusion | flops 1179648 | bytes 3542016 | tf_op jit(solution)/shard_map/mul | solution.py:378
  (77 shorter events, 2.0 us)
Async XLA Ops:
  0.6 9.4 %copy-start.1 = (bf16[128,768]{1,0:T(8,128)(2,1)S(1)}, bf16[128,768]{1,0:T(8,128)(2,1)}, u32[]{:S(2)}) copy-start(bf16[128,768]{1,0:T(8,128)(2,1)} %refs_4_.1) | copy-start | bytes 589828
  0.6 11.3 %collective-permute-start.1 = (bf16[128,768]{1,0:T(8,128)(2,1)}, bf16[128,768]{1,0:T(8,128)(2,1)S(1)}, u32[]{:S(2)}, u32[]{:S(2)}) collective-permute-start(bf16[128,768]{1,0:T(8,128)(2,1)} %refs_4_.1), channel_id=1, source_target_pairs={{0,16},{8,24},{16,32},{24,40},{32,48},{40,56},{48,64},{56,72},{64,... | collective-permute-start | bytes 589832 | tf_op jit(solution)/shard_map/ppermute | solution.py:37
  3.2 8.8 %collective-permute-start.2 = (bf16[128,768]{1,0:T(8,128)(2,1)}, bf16[128,768]{1,0:T(8,128)(2,1)S(1)}, u32[]{:S(2)}, u32[]{:S(2)}) collective-permute-start(bf16[128,768]{1,0:T(8,128)(2,1)} %refs_4_.1), channel_id=1, source_target_pairs={{0,112},{8,120},{16,0},{24,8},{32,16},{40,24},{48,32},{56,40},{64,... | collective-permute-start | bytes 589832 | tf_op jit(solution)/shard_map/ppermute | solution.py:37
  7.2 7.5 %collective-permute-start = (bf16[768,768]{1,0:T(8,128)(2,1)}, bf16[768,768]{1,0:T(8,128)(2,1)S(1)}, u32[]{:S(2)}, u32[]{:S(2)}) collective-permute-start(bf16[768,768]{1,0:T(8,128)(2,1)} %refs_0_.11), channel_id=1, source_target_pairs={{0,8},{8,0},{16,24},{24,16},{32,40},{40,32},{48,56},{56,48},{64,72... | collective-permute-start | bytes 3538952 | tf_op jit(solution)/shard_map/ppermute | solution.py:37
  12.0 6.4 %collective-permute-start.5 = (bf16[128,768]{1,0:T(8,128)(2,1)S(1)}, bf16[128,768]{1,0:T(8,128)(2,1)S(1)}, u32[]{:S(2)}, u32[]{:S(2)}) collective-permute-start(bf16[128,768]{1,0:T(8,128)(2,1)S(1)} %collective-permute-done.1.refs_4_), channel_id=1, source_target_pairs={{0,16},{8,24},{16,32},{24,40},{32,48},{40,56},{48,64},{56,72},{64,... | collective-permute-start | bytes 589832 | tf_op jit(solution)/shard_map/ppermute | solution.py:37
  12.0 6.4 %collective-permute-start.6 = (bf16[128,768]{1,0:T(8,128)(2,1)S(1)}, bf16[128,768]{1,0:T(8,128)(2,1)S(1)}, u32[]{:S(2)}, u32[]{:S(2)}) collective-permute-start(bf16[128,768]{1,0:T(8,128)(2,1)S(1)} %collective-permute-done.2.refs_5_), channel_id=1, source_target_pairs={{0,112},{8,120},{16,0},{24,8},{32,16},{40,24},{48,32},{56,40},{64,... | collective-permute-start | bytes 589832 | tf_op jit(solution)/shard_map/ppermute | solution.py:37
  14.7 1.3 copy-start
  18.3 6.6 %collective-permute-start.7 = (bf16[128,768]{1,0:T(8,128)(2,1)S(1)}, bf16[128,768]{1,0:T(8,128)(2,1)S(1)}, u32[]{:S(2)}, u32[]{:S(2)}) collective-permute-start(bf16[128,768]{1,0:T(8,128)(2,1)S(1)} %collective-permute-done.5.refs_4_), channel_id=1, source_target_pairs={{0,16},{8,24},{16,32},{24,40},{32,48},{40,56},{48,64},{56,72},{64,... | collective-permute-start | bytes 589832 | tf_op jit(solution)/shard_map/ppermute | solution.py:37
  18.3 6.6 %collective-permute-start.8 = (bf16[128,768]{1,0:T(8,128)(2,1)S(1)}, bf16[128,768]{1,0:T(8,128)(2,1)S(1)}, u32[]{:S(2)}, u32[]{:S(2)}) collective-permute-start(bf16[128,768]{1,0:T(8,128)(2,1)S(1)} %collective-permute-done.6.refs_5_), channel_id=1, source_target_pairs={{0,112},{8,120},{16,0},{24,8},{32,16},{40,24},{48,32},{56,40},{64,... | collective-permute-start | bytes 589832 | tf_op jit(solution)/shard_map/ppermute | solution.py:37
  21.0 7.4 %collective-permute-start.3 = (bf16[192,768]{1,0:T(8,128)(2,1)S(1)}, bf16[192,768]{1,0:T(8,128)(2,1)S(1)}, u32[]{:S(2)}, u32[]{:S(2)}) collective-permute-start(bf16[192,768]{1,0:T(8,128)(2,1)S(1)} %get-tuple-element.47), channel_id=1, source_target_pairs={{0,128},{8,136},{16,144},{24,152},{32,160},{40,168},{48,176},{56,1... | collective-permute-start | bytes 884744 | tf_op jit(solution)/shard_map/ppermute | solution.py:37
  22.3 8.3 %collective-permute-start.4 = (bf16[192,768]{1,0:T(8,128)(2,1)S(1)}, bf16[192,768]{1,0:T(8,128)(2,1)S(1)}, u32[]{:S(2)}, u32[]{:S(2)}) collective-permute-start(bf16[192,768]{1,0:T(8,128)(2,1)S(1)} %get-tuple-element.48), channel_id=1, source_target_pairs={{0,129},{8,137},{16,145},{24,153},{32,161},{40,169},{48,177},{56,1... | collective-permute-start | bytes 884744 | tf_op jit(solution)/shard_map/ppermute | solution.py:37
  24.9 7.6 %collective-permute-start.11 = (bf16[64,768]{1,0:T(8,128)(2,1)S(1)}, bf16[64,768]{1,0:T(8,128)(2,1)S(1)}, u32[]{:S(2)}, u32[]{:S(2)}) collective-permute-start(bf16[64,768]{1,0:T(8,128)(2,1)S(1)} %get-tuple-element.109), channel_id=1, source_target_pairs={{0,16},{8,24},{16,32},{24,40},{32,48},{40,56},{48,64},{56,72},{64,... | collective-permute-start | bytes 294920 | tf_op jit(solution)/shard_map/ppermute | solution.py:37
  25.6 7.0 %collective-permute-start.12 = (bf16[64,768]{1,0:T(8,128)(2,1)S(1)}, bf16[64,768]{1,0:T(8,128)(2,1)S(1)}, u32[]{:S(2)}, u32[]{:S(2)}) collective-permute-start(bf16[64,768]{1,0:T(8,128)(2,1)S(1)} %get-tuple-element.110), channel_id=1, source_target_pairs={{0,112},{8,120},{16,0},{24,8},{32,16},{40,24},{48,32},{56,40},{64,... | collective-permute-start | bytes 294920 | tf_op jit(solution)/shard_map/ppermute | solution.py:37
  27.8 4.7 %copy-start.2 = (s32[1024]{0:T(1024)S(1)}, s32[1024]{0:T(1024)}, u32[]{:S(2)}) copy-start(s32[1024]{0:T(1024)} %param.7) | copy-start | bytes 12292
  27.9 9.4 %collective-permute-start.9 = (bf16[256,768]{1,0:T(8,128)(2,1)S(1)}, bf16[256,768]{1,0:T(8,128)(2,1)S(1)}, u32[]{:S(2)}, u32[]{:S(2)}) collective-permute-start(bf16[256,768]{1,0:T(8,128)(2,1)S(1)} %pad_maximum_fusion), channel_id=1, source_target_pairs={{0,128},{8,136},{16,144},{24,152},{32,160},{40,168},{48,176},{56,1... | collective-permute-start | bytes 1179656 | tf_op jit(solution)/shard_map/ppermute | solution.py:37
  28.4 8.8 %collective-permute-start.10 = (bf16[256,768]{1,0:T(8,128)(2,1)S(1)}, bf16[256,768]{1,0:T(8,128)(2,1)S(1)}, u32[]{:S(2)}, u32[]{:S(2)}) collective-permute-start(bf16[256,768]{1,0:T(8,128)(2,1)S(1)} %pad_maximum_fusion.1), channel_id=1, source_target_pairs={{0,129},{8,137},{16,145},{24,153},{32,161},{40,169},{48,177},{56,1... | collective-permute-start | bytes 1179656 | tf_op jit(solution)/shard_map/ppermute | solution.py:37
  33.1 3.9 %copy-start.3 = (s32[128]{0:T(128)S(1)}, s32[128]{0:T(128)}, u32[]{:S(2)}) copy-start(s32[128]{0:T(128)} %param.6) | copy-start | bytes 1540
  33.1 6.1 %collective-permute-start.13 = (bf16[64,768]{1,0:T(8,128)(2,1)S(1)}, bf16[64,768]{1,0:T(8,128)(2,1)S(1)}, u32[]{:S(2)}, u32[]{:S(2)}) collective-permute-start(bf16[64,768]{1,0:T(8,128)(2,1)S(1)} %collective-permute-done.11.refs_4_), channel_id=1, source_target_pairs={{0,128},{8,136},{16,144},{24,152},{32,160},{40,168},{48,176},{56,1... | collective-permute-start | bytes 294920 | tf_op jit(solution)/shard_map/ppermute | solution.py:37
  33.2 6.0 %collective-permute-start.14 = (bf16[64,768]{1,0:T(8,128)(2,1)S(1)}, bf16[64,768]{1,0:T(8,128)(2,1)S(1)}, u32[]{:S(2)}, u32[]{:S(2)}) collective-permute-start(bf16[64,768]{1,0:T(8,128)(2,1)S(1)} %collective-permute-done.12.refs_5_), channel_id=1, source_target_pairs={{0,129},{8,137},{16,145},{24,153},{32,161},{40,169},{48,177},{56,1... | collective-permute-start | bytes 294920 | tf_op jit(solution)/shard_map/ppermute | solution.py:37
  41.0 3.5 %collective-permute-start.15 = (f32[3,8,128]{2,1,0:T(8,128)S(1)}, f32[3,8,128]{2,1,0:T(8,128)S(1)}, u32[]{:S(2)}, u32[]{:S(2)}) collective-permute-start(f32[3,8,128]{2,1,0:T(8,128)S(1)} %get-tuple-element.123), channel_id=1, source_target_pairs={{0,129},{8,137},{16,145},{24,153},{32,161},{40,169},{48,177},{56,1... | collective-permute-start | bytes 36872 | tf_op jit(solution)/shard_map/ppermute | solution.py:37
  43.7 3.8 %collective-permute-start.16 = (f32[3,8,128]{2,1,0:T(8,128)S(1)}, f32[3,8,128]{2,1,0:T(8,128)S(1)}, u32[]{:S(2)}, u32[]{:S(2)}) collective-permute-start(f32[3,8,128]{2,1,0:T(8,128)S(1)} %get-tuple-element.124), channel_id=1, source_target_pairs={{0,128},{8,136},{16,144},{24,152},{32,160},{40,168},{48,176},{56,1... | collective-permute-start | bytes 36872 | tf_op jit(solution)/shard_map/ppermute | solution.py:37
  64.2 12.8 %collective-permute-start.17 = (f32[8,104,768]{2,1,0:T(8,128)S(1)}, f32[8,104,768]{2,1,0:T(8,128)S(1)}, u32[]{:S(2)}, u32[]{:S(2)}) collective-permute-start(f32[8,104,768]{2,1,0:T(8,128)S(1)} %get-tuple-element.87), channel_id=1, source_target_pairs={{0,8},{8,0},{16,24},{24,16},{32,40},{40,32},{48,56},{56,48},{64,72... | collective-permute-start | bytes 7667720 | tf_op jit(solution)/shard_map/ppermute | solution.py:37
  72.5 4.4 %collective-permute-start.18 = (f32[8,128]{1,0:T(8,128)S(1)}, f32[8,128]{1,0:T(8,128)S(1)}, u32[]{:S(2)}, u32[]{:S(2)}) collective-permute-start(f32[8,128]{1,0:T(8,128)S(1)} %get-tuple-element.89), channel_id=1, source_target_pairs={{0,8},{8,0},{16,24},{24,16},{32,40},{40,32},{48,56},{56,48},{64,72... | collective-permute-start | bytes 12296 | tf_op jit(solution)/shard_map/ppermute | solution.py:37
  78.8 23.5 %all-to-all-start.1 = ((f16[8,627,128]{2,1,0:T(8,128)(2,1)}), f16[8,627,128]{2,1,0:T(8,128)(2,1)S(1)}, u32[]{:S(2)}, u32[]{:S(2)}) async-start(f16[8,627,128]{2,1,0:T(8,128)(2,1)} %convert_element_type.76), calls=%async_computation.1 | async-start | bytes 2588672 | tf_op jit(solution)/shard_map/all_to_all | solution.py:344
